TPU v7x, 512 devices: a whole 4x8x8 slice. The times are simulated.
512 devices in a mesh: dp: 32 (over y, x), tensor: 16 (over z, core).
Axes of the slice: x: 4, y: 8, z: 8, core: 2. Of those that a mesh axis runs over, the one named last changes fastest.
Arguments:
- queries: bfloat16 [2, 768, 5, 8192], P(None, 'dp', None, 'tensor'), may hold values from -400 to 400
- kv_cache: bfloat16 [2, 131072, 1024], P(None, ('dp', 'tensor')), may hold values from -6 to 6
- new_kv: bfloat16 [2, 2, 768, 5, 1024], P(None, None, 'dp', None, 'tensor'), may hold values from -6 to 6
- lengths: int32 [32, 24], P('dp'), may hold values from 1 to 341, 4096 in all within a row
- accepted: int32 [2, 768], replicated, may hold values from 0 to 4
- dest: int32 [768], replicated, may hold values from 0 to 767, as said below
Outputs:
- attended: bfloat16 [2, 768, 5, 8192], P(None, 'dp', None, 'tensor')
Inputs may be any that keep to these rules, and one draw needn't show every extreme that they name: `dest`: every slot is named by one row; the rows of one replica name at most 2 slots of any one group, and exactly 2 of each group they name. Each group's lengths sum to 4096.
All inputs are finite; a program needn't handle non-finite values.
Results may differ from a plain program's by a relative error of at most 0.002.
Values may be sent and summed in bfloat16 or wider, within the bound.
No kernel may reach another device: no remote copies, remote signals or barrier semaphores. Data moves between devices by JAX's collectives and lax.ppermute only.
A program may use at most 128 MiB of HBM per device.

v0:
```python
import jax
import jax.numpy as jnp
from jax import lax
from jax.sharding import PartitionSpec as P

HQ = 64
KVH = 8
HD = 128


def row_partials(q_row, keys, values, position, lower, upper, scale_factor):
    count = keys.shape[0]
    shape = q_row.shape[:-1]

    def compute(unused):
        top0 = jnp.full(shape, -1e30, jnp.float32)
        sum0 = jnp.zeros(shape, jnp.float32)
        acc0 = jnp.zeros(q_row.shape, jnp.float32)

        def advance(carry, index):
            top, total, accum = carry
            mask_blk = ((position >= lower) & (position < upper))[None, None, None, :]
            scores = (
                jnp.einsum("qgrd,pgd->qgrp", q_row, keys, preferred_element_type=jnp.float32)
                * scale_factor
            )
            scores = jnp.where(mask_blk, scores, -1e30)
            newtop = jnp.maximum(top, jnp.max(scores, axis=-1))
            weights = jnp.where(mask_blk, jnp.exp(scores - newtop[..., None]), 0.0)
            factor = jnp.exp(top - newtop)
            total = total * factor + jnp.sum(weights, axis=-1)
            accum = accum * factor[..., None] + jnp.einsum(
                "qgrp,pgd->qgrd",
                weights,
                values.astype(jnp.float32),
                precision=lax.Precision.HIGHEST,
            )
            return ((newtop, total, accum), None)

        result, unused2 = lax.scan(advance, (top0, sum0, acc0), jnp.arange(count // count))
        return result

    def skip(unused):
        return (
            jnp.full(shape, -1e30, jnp.float32),
            jnp.zeros(shape, jnp.float32),
            jnp.zeros(q_row.shape, jnp.float32),
        )

    touched = jnp.any((position >= lower) & (position < upper))
    return lax.cond(touched, compute, skip, 0)


def body(queries, kv_cache, new_kv, lengths, accepted, dest):
    n_dp = lax.axis_size("dp")
    n_ten = lax.axis_size("tensor")
    me_dp = lax.axis_index("dp")
    me_ten = lax.axis_index("tensor")
    steps, rd, stretch, qcols = queries.shape
    kvcols = new_kv.shape[-1]
    repeat = HQ // KVH
    per_dev = HQ // n_ten
    scale_factor = HD ** (-0.5)
    cap = max(2, rd // n_dp)
    width = n_dp * cap
    rows = dest.shape[0]
    group_of = dest // rd
    slot_of = dest % rd
    source_of = jnp.arange(rows) // rd
    group_grid = group_of.reshape(n_dp, rd)
    places = jnp.arange(rd)
    earlier = (group_grid[:, :, None] == group_grid[:, None, :]) & (
        places[None, None, :] < places[None, :, None]
    )
    rank = jnp.sum(earlier.astype(jnp.int32), axis=2).reshape(rows)
    send_key = (group_of * cap + rank).reshape(n_dp, rd)
    recv_key = source_of * cap + rank
    local_key = lax.dynamic_slice_in_dim(send_key, me_dp, 1, 0)[0]
    send_map = (jnp.arange(width)[:, None] == local_key[None, :]).astype(jnp.bfloat16)
    mine = ((slot_of[None, :] == places[:, None]) & (group_of[None, :] == me_dp)).astype(
        jnp.float32
    )
    keyed = (recv_key[:, None] == jnp.arange(width)[None, :]).astype(jnp.float32)
    place_map = jnp.dot(mine, keyed).astype(jnp.bfloat16)
    taken = jnp.dot(mine, accepted.T.astype(jnp.float32)).astype(jnp.int32)
    q_rows = jnp.transpose(queries, (1, 0, 2, 3)).reshape(rd, -1)
    kv_rows = jnp.transpose(new_kv, (2, 0, 1, 3, 4)).reshape(rd, -1)
    q_send = (
        jnp.dot(send_map, q_rows, preferred_element_type=jnp.float32)
        .astype(jnp.bfloat16)
        .reshape(n_dp, cap, -1)
    )
    kv_send = (
        jnp.dot(send_map, kv_rows, preferred_element_type=jnp.float32)
        .astype(jnp.bfloat16)
        .reshape(n_dp, cap, -1)
    )
    q_recv, kv_recv = (
        lax.all_to_all(q_send, "dp", split_axis=0, concat_axis=0, tiled=True),
        lax.all_to_all(kv_send, "dp", split_axis=0, concat_axis=0, tiled=True),
    )
    q_slot = jnp.dot(
        place_map, q_recv.reshape(width, -1), preferred_element_type=jnp.float32
    ).astype(jnp.bfloat16)
    kv_slot = jnp.dot(
        place_map, kv_recv.reshape(width, -1), preferred_element_type=jnp.float32
    ).astype(jnp.bfloat16)
    q_slot = q_slot.reshape(rd, steps, stretch, qcols)
    kv_slot = kv_slot.reshape(rd, 2, steps, stretch, kvcols)
    q_full, kv_full = (
        lax.all_gather(q_slot, "tensor", axis=3, tiled=True),
        lax.all_gather(kv_slot, "tensor", axis=4, tiled=True),
    )
    nquery = rd * steps * stretch
    seq_q = steps * stretch
    local_len = lengths[0]
    starts = jnp.cumsum(local_len) - local_len
    ends = starts + local_len
    span = kv_cache.shape[1]
    position = me_ten * span + jnp.arange(span)
    key_all = kv_cache[0].reshape(span, KVH, HD)
    val_all = kv_cache[1].reshape(span, KVH, HD)
    q_byrow = q_full.reshape(rd, seq_q, KVH, repeat, HD)

    def per_row(items):
        q_row, low, high = items
        return row_partials(q_row, key_all, val_all, position, low, high, scale_factor)

    top, total, accum = lax.map(per_row, (q_byrow, starts, ends))
    top = top.reshape(1, nquery, HQ)
    total = total.reshape(1, nquery, HQ)
    accum = accum.reshape(1, nquery, HQ, HD)
    got_acc, got_top, got_sum = (
        lax.all_to_all(accum, "tensor", split_axis=2, concat_axis=0, tiled=True),
        lax.all_to_all(top, "tensor", split_axis=2, concat_axis=0, tiled=True),
        lax.all_to_all(total, "tensor", split_axis=2, concat_axis=0, tiled=True),
    )
    best = jnp.max(got_top, axis=0)
    factor = jnp.exp(got_top - best[None])
    own = (best, jnp.sum(got_sum * factor, axis=0), jnp.sum(got_acc * factor[..., None], axis=0))
    q_own = lax.dynamic_slice_in_dim(
        q_full.reshape(rd, seq_q, HQ, HD), me_ten * per_dev, per_dev, 2
    )
    kv_heads = kv_full.reshape(rd, 2, seq_q, KVH, HD)
    head_kv = (me_ten * per_dev + jnp.arange(per_dev)) // repeat
    stretch_kv = jnp.take(kv_heads, head_kv, axis=3)
    stretch_scores = (
        jnp.einsum("rqhd,rkhd->rqhk", q_own, stretch_kv[:, 0], preferred_element_type=jnp.float32)
        * scale_factor
    )
    step_q = jnp.arange(seq_q) // stretch
    pos_q = jnp.arange(seq_q) % stretch
    same = (step_q[None, :] == step_q[:, None]) & (pos_q[None, :] <= pos_q[:, None])
    limit = jnp.take(taken, step_q, axis=1)
    before = (step_q[None, None, :] < step_q[None, :, None]) & (
        pos_q[None, None, :] <= limit[:, None, :]
    )
    stretch_valid = (same[None] | before)[:, :, None, :]
    stretch_scores = jnp.where(stretch_valid, stretch_scores, -1e30)
    cache_top = own[0].reshape(rd, seq_q, per_dev)
    cache_sum = own[1].reshape(rd, seq_q, per_dev)
    cache_acc = own[2].reshape(rd, seq_q, per_dev, HD)
    best = jnp.maximum(cache_top, jnp.max(stretch_scores, axis=-1))
    weights = jnp.where(stretch_valid, jnp.exp(stretch_scores - best[..., None]), 0.0)
    factor = jnp.exp(cache_top - best)
    total = cache_sum * factor + jnp.sum(weights, axis=-1)
    summed = cache_acc * factor[..., None] + jnp.einsum(
        "rqhk,rkhd->rqhd",
        weights,
        stretch_kv[:, 1].astype(jnp.float32),
        precision=lax.Precision.HIGHEST,
    )
    result = (summed / total[..., None]).reshape(rd, steps, stretch, per_dev * HD)
    keep = jnp.arange(stretch)[None, None, :] <= taken[:, :, None]
    result = jnp.where(keep[..., None], result, 0.0).astype(jnp.bfloat16)
    back_send = jnp.dot(
        place_map.T, result.reshape(rd, -1), preferred_element_type=jnp.float32
    ).astype(jnp.bfloat16)
    back_recv = lax.all_to_all(
        back_send.reshape(n_dp, cap, -1), "dp", split_axis=0, concat_axis=0, tiled=True
    )
    finished = jnp.dot(
        send_map.T, back_recv.reshape(width, -1), preferred_element_type=jnp.float32
    ).astype(jnp.bfloat16)
    return jnp.transpose(finished.reshape(rd, steps, stretch, per_dev * HD), (1, 0, 2, 3))


def solution(mesh):
    return jax.shard_map(
        body,
        mesh=mesh,
        in_specs=(
            P(None, "dp", None, "tensor"),
            P(None, ("dp", "tensor"), None),
            P(None, None, "dp", None, "tensor"),
            P("dp", None),
            P(),
            P(),
        ),
        out_specs=P(None, "dp", None, "tensor"),
        check_vma=False,
    )
```

profile of v0, /device:TPU:2, one launch (start us, length us, event | category | flops | bytes accessed | tf_op | source)
XLA Modules:
  0.0 566.0 jit_solution(15674199672525760992)
XLA Ops:
  10.7 10.2 %all-to-all-start = ((bf16[32,2,5120]{2,1,0:T(2,128)(2,1)}), bf16[32,2,5120]{2,1,0:T(2,128)(2,1)S(1)}, u32[]{:S(2)}, u32[]{:S(2)}) async-start(bf16[32,2,5120]{2,1,0:T(2,128)(2,1)} %reshape.508), calls=%async_computation | async-start | bytes 1310720 | tf_op jit(solution)/shard_map/all_to_all | solution.py:99
  22.0 18.6 %all-to-all-done = bf16[32,2,5120]{2,1,0:T(2,128)(2,1)S(1)} async-done(((bf16[32,2,5120]{2,1,0:T(2,128)(2,1)}), bf16[32,2,5120]{2,1,0:T(2,128)(2,1)S(1)}, u32[]{:S(2)}, u32[]{:S(2)}) %all-to-all-start) | async-done | bytes 655392 | tf_op jit(solution)/shard_map/all_to_all | solution.py:99
  43.4 5.6 all-to-all-start.3
  50.3 41.4 %all-gather.2.cloned.1.call-done = bf16[24,2,5,8192]{3,2,1,0:T(8,128)(2,1)} async-done(((bf16[24,2,5,512]{3,2,1,0:T(8,128)(2,1)}), bf16[24,2,5,8192]{3,2,1,0:T(8,128)(2,1)}) %all-gather.2.cloned.1.call-update) | async-done | bytes 3932176 | tf_op jit(solution)/shard_map/all_gather | solution.py:111
  91.8 10.2 %reshape.546 = bf16[24,10,8,8,128]{4,3,2,1,0:T(8,128)(2,1)} reshape(bf16[24,2,5,8192]{3,2,1,0:T(8,128)(2,1)} %all-gather.2.cloned.1.call-done) | data formatting | bytes 7864320 | tf_op jit(solution)/shard_map/reshape | solution.py:123
  101.9 4.8 copy.147
  106.7 130.9 %while.15 = (s32[]{:T(128)}, f32[24,10,8,8]{1,0,3,2:T(8,128)S(1)}, f32[24,10,8,8]{1,0,3,2:T(8,128)S(1)}, f32[24,10,8,8,128]{4,3,2,1,0:T(8,128)}, s32[24]{0:T(128...) while((s32[]{:T(128)}, f32[24,10,8,8]{1,0,3,2:T(8,128)S(1)}, ...), condition=%wide.region_8.9_spmd.clone, body=%wide.region_2.8_spmd.clone.sunk | while | flops 294999424 | bytes 4217091 | solution.py:129
  108.0 2.0 and_reduce_fusion.2
  110.6 3.5 conditional.3
  110.7 1.3 compare_and_fusion
  111.9 1.3 fusion.55
  116.7 2.0 and_reduce_fusion.2
  122.1 2.0 and_reduce_fusion.2
  127.4 2.0 and_reduce_fusion.2
  132.7 2.0 and_reduce_fusion.2
  138.0 2.0 and_reduce_fusion.2
  143.3 2.0 and_reduce_fusion.2
  148.6 2.0 and_reduce_fusion.2
  153.9 2.0 and_reduce_fusion.2
  159.2 2.0 and_reduce_fusion.2
  164.5 2.0 and_reduce_fusion.2
  169.8 2.0 and_reduce_fusion.2
  175.2 2.0 and_reduce_fusion.2
  180.5 2.0 and_reduce_fusion.2
  185.8 2.0 and_reduce_fusion.2
  191.1 2.0 and_reduce_fusion.2
  196.4 2.0 and_reduce_fusion.2
  201.7 2.0 and_reduce_fusion.2
  207.0 2.0 and_reduce_fusion.2
  212.3 2.0 and_reduce_fusion.2
  217.6 2.0 and_reduce_fusion.2
  222.9 2.0 and_reduce_fusion.2
  228.2 2.0 and_reduce_fusion.2
  233.6 2.0 and_reduce_fusion.2
  237.6 1.1 reshape.547
  238.7 12.6 %all-to-all-start.2 = ((f32[1,240,64]{1,0,2:T(1,128)}), f32[1,240,64]{1,0,2:T(1,128)S(1)}, u32[]{:S(2)}, u32[]{:S(2)}) async-start(f32[1,240,64]{1,0,2:T(1,128)} %reshape.547), calls=%async_computation.2 | async-start | bytes 131072 | tf_op jit(solution)/shard_map/all_to_all | solution.py:135
  251.3 1.1 reshape.549
  252.4 6.7 %all-to-all-done.2 = f32[1,240,64]{1,0,2:T(1,128)S(1)} async-done(((f32[1,240,64]{1,0,2:T(1,128)}), f32[1,240,64]{1,0,2:T(1,128)S(1)}, u32[]{:S(2)}, u32[]{:S(2)}) %all-to-all-start.2) | async-done | bytes 61472 | tf_op jit(solution)/shard_map/all_to_all | solution.py:135
  259.1 3.7 all-to-all-start.4
  262.8 10.9 %copy.151 = f32[1,240,64,128]{3,1,0,2:T(8,128)} copy(f32[1,240,64,128]{3,2,1,0:T(8,128)} %bitcast.129) | data formatting | bytes 15728640 | tf_op jit(solution)/shard_map/reshape | solution.py:132
  273.7 7.1 %all-to-all-start.1 = ((f32[1,240,64,128]{3,1,0,2:T(8,128)}), f32[1,240,64,128]{3,1,0,2:T(8,128)}, u32[]{:S(2)}, u32[]{:S(2)}) async-start(f32[1,240,64,128]{3,1,0,2:T(8,128)} %copy.151), calls=%async_computation.1 | async-start | bytes 15728640 | tf_op jit(solution)/shard_map/all_to_all | solution.py:134
  284.3 204.6 %all_gather.7 = bf16[24,2,2,5,1024]{0,2,3,1,4:T(2,128)(2,1)} all-gather(bf16[24,2,2,5,64]{0,2,3,1,4:T(2,128)(2,1)S(1)} %copy.157), channel_id=1, replica_groups=mesh['dp'=32,'tensor'=16] {'tensor'}, dimensions={4}, use_global_device_ids=true | all-gather | bytes 1044480 | tf_op jit(solution)/shard_map/all_gather | solution.py:112
  489.0 9.6 %copy.158 = bf16[24,2,2,5,1024]{4,0,3,2,1:T(8,128)(2,1)S(1)} copy(bf16[24,2,2,5,1024]{0,2,3,1,4:T(2,128)(2,1)} %all_gather.7) | data formatting | bytes 1966080 | tf_op jit(solution)/shard_map/all_gather | solution.py:112
  499.8 10.2 %reshape.548 = bf16[24,10,64,128]{3,2,1,0:T(8,128)(2,1)} reshape(bf16[24,2,5,8192]{3,2,1,0:T(8,128)(2,1)} %all-gather.2.cloned.1.call-done) | data formatting | bytes 7864320 | tf_op jit(solution)/shard_map/reshape | solution.py:142
  510.0 1.2 constant_dynamic-slice_fusion
  513.1 5.1 multiply_reduce_fusion
  518.3 1.1 fusion.20
  520.4 37.1 %all_to_all.69 = bf16[32,2,5120]{2,1,0:T(2,128)(2,1)S(1)} all-to-all(bf16[32,2,5120]{2,1,0:T(2,128)(2,1)S(1)} %reshape.525), channel_id=1, replica_groups=mesh['dp'=32,'tensor'=16] {'dp'}, dimensions={0} | all-to-all | bytes 1310720 | tf_op jit(solution)/shard_map/all_to_all | solution.py:179
  (387 shorter events, 82.9 us)
Async XLA Ops:
  6.5 35.6 %copy-start.2 = (bf16[2,2,24,5,64]{4,2,3,1,0:T(8,128)(2,1)S(1)}, bf16[2,2,24,5,64]{4,2,3,1,0:T(8,128)(2,1)}, u32[]{:S(2)}) copy-start(bf16[2,2,24,5,64]{4,2,3,1,0:T(8,128)(2,1)} %param.12) | copy-start | bytes 184324
  6.5 42.5 %copy-start = (bf16[2,256,1024]{2,1,0:T(8,128)(2,1)S(1)}, bf16[2,256,1024]{2,1,0:T(8,128)(2,1)}, u32[]{:S(2)}) copy-start(bf16[2,256,1024]{2,1,0:T(8,128)(2,1)} %param.11) | copy-start | bytes 3145732
  7.9 42.1 %copy-start.3 = (s32[1,24]{1,0:T(1,128)S(1)}, s32[1,24]{1,0:T(1,128)}, u32[]{:S(2)}) copy-start(s32[1,24]{1,0:T(1,128)} %param.13) | copy-start | bytes 292
  10.7 29.9 %all-to-all-start = ((bf16[32,2,5120]{2,1,0:T(2,128)(2,1)}), bf16[32,2,5120]{2,1,0:T(2,128)(2,1)S(1)}, u32[]{:S(2)}, u32[]{:S(2)}) async-start(bf16[32,2,5120]{2,1,0:T(2,128)(2,1)} %reshape.508), calls=%async_computation | async-start | bytes 1310720 | tf_op jit(solution)/shard_map/all_to_all | solution.py:99
  21.0 70.8 %all-gather.2.cloned.1.call-start = ((), (), s32[]{:S(2)}) async-start(), calls=%async_computation.6 | async-start | bytes 6684672 | tf_op jit(solution)/shard_map/all_gather | solution.py:111
  43.4 195.3 %all-to-all-start.3 = ((bf16[32,2,1280]{2,1,0:T(2,128)(2,1)}), bf16[32,2,1280]{2,1,0:T(2,128)(2,1)}, u32[]{:S(2)}, u32[]{:S(2)}) async-start(bf16[32,2,1280]{2,1,0:T(2,128)(2,1)} %reshape.517), calls=%async_computation.3 | async-start | bytes 327680 | tf_op jit(solution)/shard_map/all_to_all | solution.py:100
  50.3 56.4 %copy-start.1 = (f32[24,10,8,8]{1,0,3,2:T(8,128)S(1)}, f32[24,10,8,8]{1,0,3,2:T(8,128)}, u32[]{:S(2)}) copy-start(f32[24,10,8,8]{1,0,3,2:T(8,128)} %custom-call.5) | copy-start | bytes 184324
  238.7 20.4 %all-to-all-start.2 = ((f32[1,240,64]{1,0,2:T(1,128)}), f32[1,240,64]{1,0,2:T(1,128)S(1)}, u32[]{:S(2)}, u32[]{:S(2)}) async-start(f32[1,240,64]{1,0,2:T(1,128)} %reshape.547), calls=%async_computation.2 | async-start | bytes 131072 | tf_op jit(solution)/shard_map/all_to_all | solution.py:135
  259.1 14.6 %all-to-all-start.4 = ((f32[1,240,64]{1,0,2:T(1,128)}), f32[1,240,64]{1,0,2:T(1,128)S(1)}, u32[]{:S(2)}, u32[]{:S(2)}) async-start(f32[1,240,64]{1,0,2:T(1,128)} %reshape.549), calls=%async_computation.4 | async-start | bytes 131072 | tf_op jit(solution)/shard_map/all_to_all | solution.py:136
  273.7 7.2 %copy-start.4 = (s32[2,768]{1,0:T(2,128)S(1)}, s32[2,768]{1,0:T(2,128)}, u32[]{:S(2)}) copy-start(s32[2,768]{1,0:T(2,128)} %param.14) | copy-start | bytes 18436
  273.7 239.3 %all-to-all-start.1 = ((f32[1,240,64,128]{3,1,0,2:T(8,128)}), f32[1,240,64,128]{3,1,0,2:T(8,128)}, u32[]{:S(2)}, u32[]{:S(2)}) async-start(f32[1,240,64,128]{3,1,0,2:T(8,128)} %copy.151), calls=%async_computation.1 | async-start | bytes 15728640 | tf_op jit(solution)/shard_map/all_to_all | solution.py:134
Sparse Core Ops, SparseCore 0:
  42.3 49.4 all-gather.1
where the time goes:
time: 568 us; the launch traced here: 566 us
  blocking collectives  242 us (43%)
  local copies, waits for them, and re-layouts  124 us (22%)
  waiting for transfers between devices  66.7 us (12%)
  other arithmetic  57 us (10%)
  starting transfers between devices  39.3 us (7%)
  loops' own time  18.1 us (3%)
  between operations  13.9 us (2%)
    all_gather x1, blocking collectives, body(): lax.all_gather(kv_slot, 'tensor', axis=4, tiled=True)  205 us
    reduce_or x24, other arithmetic, row_partials(): touched = jnp.any((position >= lower) & (position < upper))  47.3 us
    all_gather x1, waiting for transfers between devices, body(): lax.all_gather(q_slot, 'tensor', axis=3, tiled=True)  41.4 us
    all_to_all x1, blocking collectives, body(): lax.all_to_all(back_send.reshape(n_dp, cap, -1), 'dp', split_axis=0, conc...  37.1 us
    dynamic_update_slice x120, local copies, waits for them, and re-layouts, body(): top, total, accum = lax.map(per_row, (q_byrow, starts, ends))  30.9 us
    dynamic_slice x48, local copies, waits for them, and re-layouts, body(): top, total, accum = lax.map(per_row, (q_byrow, starts, ends))  30.3 us
    all_to_all x1, waiting for transfers between devices, body(): lax.all_to_all(q_send, 'dp', split_axis=0, concat_axis=0, tiled=True)  18.6 us
    another operation x1, loops' own time, body(): top, total, accum = lax.map(per_row, (q_byrow, starts, ends))  17.2 us
  transfers between devices with their start and end apart: 6, of which 3 were waited for; matrix products, arithmetic and copies ran while one was open for 30% of the time, Pallas kernels for 0%

commit v1 on v0

v1 whole, which is shorter than its diff:
```python
import jax
import jax.numpy as jnp
from jax import lax
from jax.experimental import pallas as pl
from jax.experimental.pallas import tpu as pltpu
from jax.sharding import PartitionSpec as P

HQ = 64
KVH = 8
HD = 128
CH = 5
STEPS = 2
RD = 24
SPAN = 256
WIN = 384
TOK = STEPS * CH
PER = 4
QR = PER * TOK
SCALE = HD**-0.5
VMEM = pltpu.MemorySpace.VMEM
SMEM = pltpu.MemorySpace.SMEM
LIMIT = 48 * 1024 * 1024


def split_cache(z, kv):
    def kernel(z_ref, kv_ref, own_ref, right_ref, left_ref, sems):
        me = z_ref[0]
        copies = []

        def send(side, dist, dst):
            col = pl.multiple_of(lax.rem(me + dist, KVH) * HD, HD)
            sem = sems.at[len(copies)]
            copies.append(
                pltpu.make_async_copy(kv_ref.at[side, :, pl.ds(col, HD)], dst, sem)
            )

        for side in range(2):
            for dist in range(1, 4):
                send(side, dist, right_ref.at[2 * (dist - 1) + side])
                send(side, KVH - dist, left_ref.at[2 * (dist - 1) + side])
            send(side, 0, own_ref.at[side])
        send(0, 4, right_ref.at[6])
        send(1, 4, left_ref.at[6])
        for copy in copies:
            copy.start()
        for copy in copies:
            copy.wait()

    return pl.pallas_call(
        kernel,
        out_shape=(
            jax.ShapeDtypeStruct((2, SPAN, HD), kv.dtype),
            jax.ShapeDtypeStruct((7, SPAN, HD), kv.dtype),
            jax.ShapeDtypeStruct((7, SPAN, HD), kv.dtype),
        ),
        in_specs=[pl.BlockSpec(memory_space=SMEM), pl.BlockSpec(memory_space=pl.ANY)],
        out_specs=[pl.BlockSpec(memory_space=pl.ANY)] * 3,
        scratch_shapes=[pltpu.SemaphoreType.DMA((16,))],
        cost_estimate=pl.CostEstimate(flops=0, bytes_accessed=2 << 20, transcendentals=0),
        name="split_cache",
    )(z, kv)


def pack_rows(pos, queries, new_kv):
    def kernel(pos_ref, q_ref, n_ref, out_ref, qs, ns):
        for j in range(RD):
            at = pos_ref[j]
            for s in range(STEPS):
                q = q_ref[s, j].astype(jnp.float32)
                for h in range(PER):
                    row = h * TOK + s * CH
                    qs[at, row : row + CH, :] = q[:, h * HD : (h + 1) * HD]
                n = jnp.concatenate([n_ref[0, s, j], n_ref[1, s, j]], axis=-1)
                ns[at, s * CH : (s + 1) * CH, :] = n.astype(jnp.float32)
        for g in range(32):
            block = [qs[2 * g], qs[2 * g + 1], ns[2 * g], ns[2 * g + 1]]
            out_ref[g] = jnp.concatenate(block, axis=0).astype(jnp.bfloat16)

    return pl.pallas_call(
        kernel,
        out_shape=jax.ShapeDtypeStruct((32, 2 * (QR + TOK), HD), jnp.bfloat16),
        in_specs=[
            pl.BlockSpec(memory_space=SMEM),
            pl.BlockSpec(memory_space=VMEM),
            pl.BlockSpec(memory_space=VMEM),
        ],
        out_specs=pl.BlockSpec(memory_space=VMEM),
        scratch_shapes=[
            pltpu.VMEM((64, QR, HD), jnp.float32),
            pltpu.VMEM((64, TOK, HD), jnp.float32),
        ],
        compiler_params=pltpu.CompilerParams(vmem_limit_bytes=LIMIT),
        cost_estimate=pl.CostEstimate(flops=0, bytes_accessed=2 << 20, transcendentals=0),
        name="pack_rows",
    )(pos, queries, new_kv)


def attend(info, received, new_sib, pieces, sib):
    n_pieces = len(pieces)
    layout = []
    for i, dist in enumerate((0, -1, 1, -2, 2, -3, 3)):
        layout += [(i, 0, 0, dist), (i, 1, 1, dist)]
    layout += [(7, 0, 0, 4), (8, 0, 1, 4)]

    def kernel(info_ref, recv_ref, ns_ref, *refs):
        piece_refs = refs[:n_pieces]
        sib_ref, out_ref, kbuf, vbuf, qs, kn, vn, sems = refs[n_pieces:]
        z, core = info_ref[5, 0], info_ref[5, 1]
        copies = []
        for unit, (i, u, side, dist) in enumerate(layout):
            src_z = lax.rem(z + dist + KVH, KVH)
            for other in range(2):
                owner = src_z * 2 + (core if other == 0 else 1 - core)
                rows = pl.ds(pl.multiple_of(owner * SPAN, SPAN), SPAN)
                src = piece_refs[i].at[u] if other == 0 else sib_ref.at[unit]
                dst = (kbuf, vbuf)[side].at[rows]
                copies.append(pltpu.make_async_copy(src, dst, sems.at[len(copies)]))
        for copy in copies:
            copy.start()
        kbuf[KVH * 2 * SPAN :, :] = jnp.zeros((WIN, HD), jnp.bfloat16)
        vbuf[KVH * 2 * SPAN :, :] = jnp.zeros((WIN, HD), jnp.bfloat16)
        low_half = lax.broadcasted_iota(jnp.int32, (TOK, HD), 1) < HD // 2
        fill = jnp.zeros((16 - TOK, HD), jnp.float32)
        for j in range(RD):
            at = info_ref[0, j]
            g, second = at // 2, lax.rem(at, 2) == 1
            block = recv_ref[g].astype(jnp.float32)
            other = ns_ref[g].astype(jnp.float32)
            qs[j] = jnp.where(second, block[QR : 2 * QR], block[:QR]).astype(jnp.bfloat16)
            base = 2 * QR
            mine = jnp.where(second, block[base + TOK :], block[base : base + TOK])
            theirs = jnp.where(second, other[TOK:], other[:TOK])
            low = jnp.where(core == 0, mine, theirs)
            high = jnp.where(core == 0, theirs, mine)
            key = jnp.where(low_half, low, pltpu.roll(high, HD // 2, 1))
            value = jnp.where(low_half, pltpu.roll(low, HD // 2, 1), high)
            kn[j] = jnp.concatenate([key, fill], axis=0).astype(jnp.bfloat16)
            vn[j] = jnp.concatenate([value, fill], axis=0).astype(jnp.bfloat16)
        col = lax.broadcasted_iota(jnp.int32, (QR, WIN), 1)
        ncol = lax.broadcasted_iota(jnp.int32, (QR, 16), 1)
        nrow = lax.rem(lax.broadcasted_iota(jnp.int32, (QR, 16), 0), TOK)
        step_k, step_q = ncol // CH, nrow // CH
        pos_k, pos_q = lax.rem(ncol, CH), lax.rem(nrow, CH)
        need = jnp.where((step_k == step_q) & (pos_k <= pos_q), -1, 100)
        need = jnp.where(step_k < step_q, pos_k, need)
        need = jnp.where(ncol < TOK, need, 100)
        trow = lax.rem(lax.broadcasted_iota(jnp.int32, (QR, HD), 0), TOK)
        tstep, tpos = trow // CH, lax.rem(trow, CH)
        for copy in copies:
            copy.wait()

        group = 6

        def some(it, carry):
            js = [it * group + i for i in range(group)]
            scores, values = [], []
            for j in js:
                start, length = info_ref[1, j], info_ref[2, j]
                base = pl.multiple_of((start // 16) * 16, 16)
                off = start - base
                keys = jnp.concatenate([kbuf[pl.ds(base, WIN), :], kn[j]], axis=0)
                sc = lax.dot_general(
                    qs[j], keys, (((1,), (1,)), ((), ())), preferred_element_type=jnp.float32
                )
                cached = jnp.where(
                    (col >= off) & (col < off + length), sc[:, :WIN] * SCALE, -1e30
                )
                fresh = jnp.where(need <= info_ref[3, j], sc[:, WIN:] * SCALE, -1e30)
                scores.append((cached, fresh))
            weights = []
            for cached, fresh in scores:
                top = jnp.maximum(
                    jnp.max(cached, axis=1, keepdims=True), jnp.max(fresh, axis=1, keepdims=True)
                )
                wc, wf = jnp.exp(cached - top), jnp.exp(fresh - top)
                total = jnp.sum(wc, axis=1, keepdims=True) + jnp.sum(wf, axis=1, keepdims=True)
                weights.append((jnp.concatenate([wc, wf], axis=1), total))
            for j, (w, total) in zip(js, weights):
                base = pl.multiple_of((info_ref[1, j] // 16) * 16, 16)
                vals = jnp.concatenate([vbuf[pl.ds(base, WIN), :], vn[j]], axis=0)
                high = w.astype(jnp.bfloat16)
                low = (w - high.astype(jnp.float32)).astype(jnp.bfloat16)
                dims = (((1,), (0,)), ((), ()))
                acc = lax.dot_general(high, vals, dims, preferred_element_type=jnp.float32)
                acc += lax.dot_general(low, vals, dims, preferred_element_type=jnp.float32)
                limit = jnp.where(tstep == 0, info_ref[3, j], info_ref[4, j])
                out = jnp.where(tpos <= limit, acc / total, 0.0)
                out_ref[info_ref[0, j]] = out.astype(jnp.bfloat16)
            return carry

        lax.fori_loop(0, RD // group, some, 0)

    return pl.pallas_call(
        kernel,
        out_shape=jax.ShapeDtypeStruct((64, QR, HD), jnp.bfloat16),
        in_specs=[
            pl.BlockSpec(memory_space=SMEM),
            pl.BlockSpec(memory_space=VMEM),
            pl.BlockSpec(memory_space=VMEM),
        ]
        + [pl.BlockSpec(memory_space=pl.ANY)] * (n_pieces + 1),
        out_specs=pl.BlockSpec(memory_space=VMEM),
        scratch_shapes=[
            pltpu.VMEM((KVH * 2 * SPAN + WIN, HD), jnp.bfloat16),
            pltpu.VMEM((KVH * 2 * SPAN + WIN, HD), jnp.bfloat16),
            pltpu.VMEM((RD, QR, HD), jnp.bfloat16),
            pltpu.VMEM((RD, 16, HD), jnp.bfloat16),
            pltpu.VMEM((RD, 16, HD), jnp.bfloat16),
            pltpu.SemaphoreType.DMA((32,)),
        ],
        compiler_params=pltpu.CompilerParams(vmem_limit_bytes=LIMIT),
        cost_estimate=pl.CostEstimate(
            flops=24 * 40 * 400 * 128 * 6, bytes_accessed=4 << 20, transcendentals=24 * 40 * 400
        ),
        name="attend",
    )(info, received, new_sib, *pieces, sib)


def unpack_rows(pos, received):
    def kernel(pos_ref, in_ref, out_ref):
        for j in range(RD):
            block = in_ref[pos_ref[j]].astype(jnp.float32)
            for s in range(STEPS):
                heads = [block[h * TOK + s * CH : h * TOK + (s + 1) * CH] for h in range(PER)]
                out_ref[s, j] = jnp.concatenate(heads, axis=1).astype(jnp.bfloat16)

    return pl.pallas_call(
        kernel,
        out_shape=jax.ShapeDtypeStruct((STEPS, RD, CH, PER * HD), jnp.bfloat16),
        in_specs=[pl.BlockSpec(memory_space=SMEM), pl.BlockSpec(memory_space=VMEM)],
        out_specs=pl.BlockSpec(memory_space=VMEM),
        compiler_params=pltpu.CompilerParams(vmem_limit_bytes=LIMIT),
        cost_estimate=pl.CostEstimate(flops=0, bytes_accessed=1 << 20, transcendentals=0),
        name="unpack_rows",
    )(pos, received)


def body(queries, kv_cache, new_kv, lengths, accepted, dest):
    me_dp = lax.axis_index("dp")
    me_ten = lax.axis_index("tensor")
    z, core = me_ten // 2, me_ten % 2
    n_dp = lax.axis_size("dp")

    def along_z(x, k):
        perm = [(t, (t // 2 + k) % KVH * 2 + t % 2) for t in range(16)]
        return lax.ppermute(x, "tensor", perm)

    def sibling(x):
        return lax.ppermute(x, "tensor", [(t, t ^ 1) for t in range(16)])

    own, right, left = split_cache(z.reshape(1).astype(jnp.int32), kv_cache)
    pieces = [own]
    for _ in range(4):
        right, left = along_z(right, 1), along_z(left, -1)
        pieces += [right[:2], left[:2]]
        right, left = right[2:], left[2:]

    group_of = dest // RD
    mine = lax.dynamic_slice_in_dim(group_of, me_dp * RD, RD)
    order = jnp.arange(RD)
    rank = jnp.sum((mine[:, None] == mine[None, :]) & (order[None, :] < order[:, None]), axis=1)
    send_pos = (mine * 2 + rank).astype(jnp.int32)
    here = (group_of == me_dp).reshape(n_dp, RD)
    before = jnp.sum(here[:, None, :] & (order[None, :] < order[:, None]), axis=2)
    place = (jnp.arange(n_dp)[:, None] * 2 + before).reshape(-1)
    hit = dest[None, :] == (me_dp * RD + order)[:, None]
    recv_pos = jnp.sum(jnp.where(hit, place[None, :], 0), axis=1)
    taken = jnp.sum(jnp.where(hit[None], accepted[:, None, :], 0), axis=2)
    length = lengths[0]
    start = jnp.sum(jnp.where(order[None, :] < order[:, None], length[None, :], 0), axis=1)
    ident = jnp.where(order == 0, z, jnp.where(order == 1, core, 0))
    info = jnp.stack([recv_pos, start, length, taken[0], taken[1], ident]).astype(jnp.int32)

    packed = pack_rows(send_pos, queries, new_kv)
    received = lax.all_to_all(packed, "dp", split_axis=0, concat_axis=0, tiled=True)
    new_sib = sibling(received[:, 2 * QR :])
    sib = sibling(jnp.concatenate(pieces, axis=0))
    outs = attend(info, received, new_sib, pieces, sib)
    back = lax.all_to_all(
        outs.reshape(n_dp, 2 * QR, HD), "dp", split_axis=0, concat_axis=0, tiled=True
    )
    return unpack_rows(send_pos, back.reshape(2 * n_dp, QR, HD))


def solution(mesh):
    return jax.shard_map(
        body,
        mesh=mesh,
        in_specs=(
            P(None, "dp", None, "tensor"),
            P(None, ("dp", "tensor"), None),
            P(None, None, "dp", None, "tensor"),
            P("dp", None),
            P(),
            P(),
        ),
        out_specs=P(None, "dp", None, "tensor"),
        check_vma=False,
    )
```

time: 568 us -> 136 us (0.24)
  blocking collectives: 242 us -> 29.8 us
  local copies, waits for them, and re-layouts: 124 us -> 8.91 us
  waiting for transfers between devices: 66.7 us -> 4.44 us
  other arithmetic: 57 us -> 0.97 us
  Pallas kernels: 0 us -> 42.1 us
  loops' own time: 18.1 us -> 0 us
  between operations: 13.9 us -> 0.37 us
  starting transfers between devices: 39.3 us -> 48.7 us
    all_gather x1 -> x0, blocking collectives: 205 us -> none  [body(): lax.all_gather(kv_slot, 'tensor', axis=4, tiled=True)]
    reduce_or x24 -> x0, other arithmetic: 47.3 us -> none  [row_partials(): touched = jnp.any((position >= lower) & (position < upper))]
    pallas_call x0 -> x4, Pallas kernels: none -> 42.1 us  [the longest x1 33 us: split_cache(): pl.pallas_call(kernel, out_shape=(jax.ShapeDtypeStruct((2, SPAN, HD), kv....]
    all_gather x1 -> x0, waiting for transfers between devices: 41.4 us -> none  [body(): lax.all_gather(q_slot, 'tensor', axis=3, tiled=True)]
    reshape x25 -> x0, local copies, waits for them, and re-layouts: 40.3 us -> none  [the longest x1 10.9 us: body(): accum = accum.reshape(1, nquery, HQ, HD)]
    ppermute x0 -> x10, starting transfers between devices: none -> 38.3 us  [the longest x8 34 us: along_z(): return lax.ppermute(x, 'tensor', perm)]
    dynamic_slice x49 -> x1, local copies, waits for them, and re-layouts: 31.4 us -> 0.08 us  [body(): mine = lax.dynamic_slice_in_dim(group_of, me_dp * RD, RD)]
    dynamic_update_slice x120 -> x0, local copies, waits for them, and re-layouts: 30.9 us -> none  [body(): top, total, accum = lax.map(per_row, (q_byrow, starts, ends))]
  transfers between devices with their start and end apart: 6 -> 11, of which waited for: 3 -> 3; matrix products, arithmetic and copies ran while one was open for 30% -> 6% of each run, Pallas kernels for 0% -> 1%
where the time goes in v1:
time: 136 us; the launch traced here: 135 us
  starting transfers between devices  48.7 us (36%)
  Pallas kernels  42.1 us (31%)
  blocking collectives  29.8 us (22%)
  local copies, waits for them, and re-layouts  8.91 us (7%)
  waiting for transfers between devices  4.44 us (3%)
    ppermute x8, starting transfers between devices, along_z(): return lax.ppermute(x, 'tensor', perm)  34 us
    pallas_call x1, Pallas kernels, split_cache(): pl.pallas_call(kernel, out_shape=(jax.ShapeDtypeStruct((2, SPAN, HD), kv....  33 us
    all_to_all x1, blocking collectives, body(): lax.all_to_all(outs.reshape(n_dp, 2 * QR, HD), 'dp', split_axis=0, concat...  29.8 us
    all_to_all x1, starting transfers between devices, body(): lax.all_to_all(packed, 'dp', split_axis=0, concat_axis=0, tiled=True)  10.4 us
    unnamed x22, local copies, waits for them, and re-layouts  6.96 us
    pallas_call x1, Pallas kernels, attend(): pl.pallas_call(kernel, out_shape=jax.ShapeDtypeStruct((64, QR, HD), jnp.b...  6.7 us
    ppermute x2, starting transfers between devices, sibling(): return lax.ppermute(x, 'tensor', [(t, t ^ 1) for t in range(16)])  4.31 us
    ppermute x8, waiting for transfers between devices, along_z(): return lax.ppermute(x, 'tensor', perm)  3.57 us
  transfers between devices with their start and end apart: 11, of which 3 were waited for; matrix products, arithmetic and copies ran while one was open for 6% of the time, Pallas kernels for 1%

profile of v1, /device:TPU:2, one launch (start us, length us, event | category | flops | bytes accessed | tf_op | source)
XLA Modules:
  0.0 135.3 jit_solution(7020051576817675348)
XLA Ops:
  0.0 33.0 %split_cache.1 = (bf16[2,256,128]{2,1,0:T(8,128)(2,1)}, bf16[7,256,128]{2,1,0:T(8,128)(2,1)}, bf16[7,256,128]{2,1,0:T(8,128)(2,1)}) custom-call(s32[1]{0:T(128)} %bitcast.3.z_ref, bf16[2,256,1024]{2,1,0:T(8,128)(2,1)} %kv_ref.1), custom_call_target="tpu_custom_call" | custom-call | bytes 2097152 | tf_op jit(solution)/shard_map/split_cache/pallas_call | solution.py:49
  33.0 4.3 %collective-permute-start.1 = (bf16[7,256,128]{2,1,0:T(8,128)(2,1)}, bf16[7,256,128]{2,1,0:T(8,128)(2,1)S(1)}, u32[]{:S(2)}, u32[]{:S(2)}) collective-permute-start(bf16[7,256,128]{2,1,0:T(8,128)(2,1)} %get-tuple-element.9), channel_id=1, source_target_pairs={{0,2},{1,3},{2,4},{3,5},{4,6},{5,7},{6,8},{7,9},{8,10},{9,11},{10,... | collective-permute-start | bytes 1376264 | tf_op jit(solution)/shard_map/ppermute | solution.py:246
  37.3 0.0 copy-start.3
  37.3 8.6 %collective-permute-start.2 = (bf16[7,256,128]{2,1,0:T(8,128)(2,1)}, bf16[7,256,128]{2,1,0:T(8,128)(2,1)S(1)}, u32[]{:S(2)}, u32[]{:S(2)}) collective-permute-start(bf16[7,256,128]{2,1,0:T(8,128)(2,1)} %get-tuple-element.10), channel_id=1, source_target_pairs={{0,14},{1,15},{2,0},{3,1},{4,2},{5,3},{6,4},{7,5},{8,6},{9,7},{10,... | collective-permute-start | bytes 1376264 | tf_op jit(solution)/shard_map/ppermute | solution.py:246
  45.9 0.1 dynamic_slice.3
  46.0 0.2 convert_reduce_fusion.1
  46.2 0.0 copy-start.2
  46.2 0.1 copy.15.q_ref
  46.3 0.8 copy-done.2
  47.2 0.1 multiply_add_fusion.pos_ref
  47.2 1.7 %pack_rows.1 = bf16[32,100,128]{2,1,0:T(8,128)(2,1)} custom-call(s32[24]{0:T(128)S(1)} %multiply_add_fusion.pos_ref, bf16[2,24,5,512]{3,2,1,0:T(8,128)(2,1)S(1)} %copy.15.q_ref, bf16[2,2,24,5,64]{4,3,2,1,0:T(8,128)(2,1)S(1)} %copy.16.n_ref), custom_call_target="tpu_custom_call" | custom-call | bytes 2097152 | tf_op jit(solution)/shard_map/pack_rows/pallas_call | solution.py:79
  49.0 10.4 %all-to-all-start = ((bf16[32,100,128]{2,1,0:T(8,128)(2,1)}), bf16[32,100,128]{2,1,0:T(8,128)(2,1)S(1)}, u32[]{:S(2)}, u32[]{:S(2)}) async-start(bf16[32,100,128]{2,1,0:T(8,128)(2,1)} %pack_rows.1), calls=%async_computation | async-start | bytes 1703936 | tf_op jit(solution)/shard_map/all_to_all | solution.py:275
  59.3 0.1 and.36
  59.4 0.1 copy.13
  59.6 0.6 constant_dynamic-update-slice_fusion.8
  60.2 0.2 convert_reduce_fusion
  60.4 1.9 %collective-permute-start.3 = (bf16[5,256,128]{2,1,0:T(8,128)(2,1)S(1)}, bf16[5,256,128]{2,1,0:T(8,128)(2,1)S(1)}, u32[]{:S(2)}, u32[]{:S(2)}) collective-permute-start(bf16[5,256,128]{2,1,0:T(8,128)(2,1)S(1)} %slice.58), channel_id=1, source_target_pairs={{0,2},{1,3},{2,4},{3,5},{4,6},{5,7},{6,8},{7,9},{8,10},{9,11},{10,... | collective-permute-start | bytes 983048 | tf_op jit(solution)/shard_map/ppermute | solution.py:246
  62.4 5.1 %collective-permute-start.4 = (bf16[5,256,128]{2,1,0:T(8,128)(2,1)S(1)}, bf16[5,256,128]{2,1,0:T(8,128)(2,1)S(1)}, u32[]{:S(2)}, u32[]{:S(2)}) collective-permute-start(bf16[5,256,128]{2,1,0:T(8,128)(2,1)S(1)} %slice.60), channel_id=1, source_target_pairs={{0,14},{1,15},{2,0},{3,1},{4,2},{5,3},{6,4},{7,5},{8,6},{9,7},{10,... | collective-permute-start | bytes 983048 | tf_op jit(solution)/shard_map/ppermute | solution.py:246
  67.5 0.7 constant_dynamic-update-slice_fusion.7
  68.2 0.7 constant_dynamic-update-slice_fusion.6
  68.9 3.2 %collective-permute-done.3 = bf16[5,256,128]{2,1,0:T(8,128)(2,1)S(1)} collective-permute-done((bf16[5,256,128]{2,1,0:T(8,128)(2,1)S(1)}, bf16[5,256,128]{2,1,0:T(8,128)(2,1)S(1)}, u32[]{:S(2)}, u32[]{:S(2)}) %collective-permute-start.3) | collective-permute-done | bytes 327712 | tf_op jit(solution)/shard_map/ppermute | solution.py:246
  72.1 1.9 %collective-permute-start.5 = (bf16[3,256,128]{2,1,0:T(8,128)(2,1)S(1)}, bf16[3,256,128]{2,1,0:T(8,128)(2,1)S(1)}, u32[]{:S(2)}, u32[]{:S(2)}) collective-permute-start(bf16[3,256,128]{2,1,0:T(8,128)(2,1)S(1)} %slice.62), channel_id=1, source_target_pairs={{0,2},{1,3},{2,4},{3,5},{4,6},{5,7},{6,8},{7,9},{8,10},{9,11},{10,... | collective-permute-start | bytes 589832 | tf_op jit(solution)/shard_map/ppermute | solution.py:246
  74.1 5.1 %collective-permute-start.6 = (bf16[3,256,128]{2,1,0:T(8,128)(2,1)S(1)}, bf16[3,256,128]{2,1,0:T(8,128)(2,1)S(1)}, u32[]{:S(2)}, u32[]{:S(2)}) collective-permute-start(bf16[3,256,128]{2,1,0:T(8,128)(2,1)S(1)} %slice.64), channel_id=1, source_target_pairs={{0,14},{1,15},{2,0},{3,1},{4,2},{5,3},{6,4},{7,5},{8,6},{9,7},{10,... | collective-permute-start | bytes 589832 | tf_op jit(solution)/shard_map/ppermute | solution.py:246
  79.2 0.7 constant_dynamic-update-slice_fusion.5
  79.9 0.7 constant_dynamic-update-slice_fusion.4
  80.6 0.3 collective-permute-done.5
  80.9 1.9 %collective-permute-start.7 = (bf16[1,256,128]{2,1,0:T(8,128)(2,1)S(1)}, bf16[1,256,128]{2,1,0:T(8,128)(2,1)S(1)}, u32[]{:S(2)}, u32[]{:S(2)}) collective-permute-start(bf16[1,256,128]{2,1,0:T(8,128)(2,1)S(1)} %slice.66), channel_id=1, source_target_pairs={{0,2},{1,3},{2,4},{3,5},{4,6},{5,7},{6,8},{7,9},{8,10},{9,11},{10,... | collective-permute-start | bytes 196616 | tf_op jit(solution)/shard_map/ppermute | solution.py:246
  82.9 5.1 %collective-permute-start.8 = (bf16[1,256,128]{2,1,0:T(8,128)(2,1)S(1)}, bf16[1,256,128]{2,1,0:T(8,128)(2,1)S(1)}, u32[]{:S(2)}, u32[]{:S(2)}) collective-permute-start(bf16[1,256,128]{2,1,0:T(8,128)(2,1)S(1)} %slice.67), channel_id=1, source_target_pairs={{0,14},{1,15},{2,0},{3,1},{4,2},{5,3},{6,4},{7,5},{8,6},{9,7},{10,... | collective-permute-start | bytes 196616 | tf_op jit(solution)/shard_map/ppermute | solution.py:246
  88.0 0.7 constant_dynamic-update-slice_fusion.3
  88.7 0.7 constant_dynamic-update-slice_fusion.2
  89.4 0.6 constant_dynamic-update-slice_fusion.1
  90.0 0.6 constant_dynamic-update-slice_fusion
  90.6 1.9 %collective-permute-start.9 = (bf16[16,256,128]{2,1,0:T(8,128)(2,1)}, bf16[16,256,128]{2,1,0:T(8,128)(2,1)S(1)}, u32[]{:S(2)}, u32[]{:S(2)}) collective-permute-start(bf16[16,256,128]{2,1,0:T(8,128)(2,1)} %constant_dynamic-update-slice_fusion), channel_id=1, source_target_pairs={{0,1},{1,0},{2,3},{3,2},{4,5},{5,4},{6,7},{7,6},{8,9},{9,8},{10,11... | collective-permute-start | bytes 3145736 | tf_op jit(solution)/shard_map/ppermute | solution.py:249
  92.6 0.1 copy.14
  92.6 0.1 add.43
  92.8 0.0 copy-start.5
  92.8 0.6 copy-done.5
  93.4 0.1 select_reduce_fusion.2
  93.5 0.2 select_reduce_fusion.1
  93.7 0.1 broadcast_compare_fusion
  93.8 0.0 copy-start.4
  93.9 2.4 %collective-permute-start = (bf16[32,20,128]{2,1,0:T(8,128)(2,1)S(1)}, bf16[32,20,128]{2,1,0:T(8,128)(2,1)S(1)}, u32[]{:S(2)}, u32[]{:S(2)}) collective-permute-start(bf16[32,20,128]{2,1,0:T(8,128)(2,1)S(1)} %slice.55), channel_id=1, source_target_pairs={{0,1},{1,0},{2,3},{3,2},{4,5},{5,4},{6,7},{7,6},{8,9},{9,8},{10,11... | collective-permute-start | bytes 491528 | tf_op jit(solution)/shard_map/ppermute | solution.py:249
  96.3 0.1 select_reduce_fusion
  96.4 0.9 collective-permute-done.ns_ref
  97.3 6.7 %attend.1 = bf16[64,40,128]{2,1,0:T(8,128)(2,1)S(1)} custom-call(s32[6,24]{1,0:T(8,128)S(1)} %stack.12.info_ref, bf16[32,100,128]{2,1,0:T(8,128)(2,1)S(1)} %all-to-all-done.recv_ref, bf16[32,20,128]{2,1,0:T(8,128)(2,1)S(1)} %collective-permute-done.ns_ref, bf16[2,256,128]{2,1,0:T(8,128)(2,1)S(1)} %copy-done, ...), custom_call_target="tpu_custom_call" | custom-call | flops 294912000 | bytes 4194304 | tf_op jit(solution)/shard_map/attend/pallas_call | solution.py:193
  104.0 29.8 %all_to_all.10 = bf16[32,80,128]{2,1,0:T(8,128)(2,1)S(1)} all-to-all(bf16[32,80,128]{2,1,0:T(8,128)(2,1)S(1)} %bitcast.7), channel_id=1, replica_groups=mesh['dp'=32,'tensor'=16] {'dp'}, dimensions={0} | all-to-all | bytes 1310720 | tf_op jit(solution)/shard_map/all_to_all | solution.py:279
  133.8 0.7 unpack_rows.1
  134.5 0.8 copy.17
  (29 shorter events, 0.2 us)
Async XLA Ops:
  0.0 46.2 %copy-start.1 = (bf16[2,24,5,512]{3,1,2,0:T(8,128)(2,1)S(1)}, bf16[2,24,5,512]{3,1,2,0:T(8,128)(2,1)}, u32[]{:S(2)}) copy-start(bf16[2,24,5,512]{3,1,2,0:T(8,128)(2,1)} %param.6) | copy-start | bytes 737284
  33.0 27.3 %collective-permute-start.1 = (bf16[7,256,128]{2,1,0:T(8,128)(2,1)}, bf16[7,256,128]{2,1,0:T(8,128)(2,1)S(1)}, u32[]{:S(2)}, u32[]{:S(2)}) collective-permute-start(bf16[7,256,128]{2,1,0:T(8,128)(2,1)} %get-tuple-element.9), channel_id=1, source_target_pairs={{0,2},{1,3},{2,4},{3,5},{4,6},{5,7},{6,8},{7,9},{8,10},{9,11},{10,... | collective-permute-start | bytes 1376264 | tf_op jit(solution)/shard_map/ppermute | solution.py:246
  37.3 8.6 %copy-start.3 = (s32[768]{0:T(1024)S(1)}, s32[768]{0:T(1024)}, u32[]{:S(2)}) copy-start(s32[768]{0:T(1024)} %param.11) | copy-start | bytes 9220
  37.3 25.0 %collective-permute-start.2 = (bf16[7,256,128]{2,1,0:T(8,128)(2,1)}, bf16[7,256,128]{2,1,0:T(8,128)(2,1)S(1)}, u32[]{:S(2)}, u32[]{:S(2)}) collective-permute-start(bf16[7,256,128]{2,1,0:T(8,128)(2,1)} %get-tuple-element.10), channel_id=1, source_target_pairs={{0,14},{1,15},{2,0},{3,1},{4,2},{5,3},{6,4},{7,5},{8,6},{9,7},{10,... | collective-permute-start | bytes 1376264 | tf_op jit(solution)/shard_map/ppermute | solution.py:246
  46.2 0.9 copy-start.2
  49.0 10.6 %copy-start = (bf16[2,256,128]{2,1,0:T(8,128)(2,1)S(1)}, bf16[2,256,128]{2,1,0:T(8,128)(2,1)}, u32[]{:S(2)}) copy-start(bf16[2,256,128]{2,1,0:T(8,128)(2,1)} %get-tuple-element.8.refs_0_) | copy-start | bytes 393220
  49.0 44.9 %all-to-all-start = ((bf16[32,100,128]{2,1,0:T(8,128)(2,1)}), bf16[32,100,128]{2,1,0:T(8,128)(2,1)S(1)}, u32[]{:S(2)}, u32[]{:S(2)}) async-start(bf16[32,100,128]{2,1,0:T(8,128)(2,1)} %pack_rows.1), calls=%async_computation | async-start | bytes 1703936 | tf_op jit(solution)/shard_map/all_to_all | solution.py:275
  60.4 11.7 %collective-permute-start.3 = (bf16[5,256,128]{2,1,0:T(8,128)(2,1)S(1)}, bf16[5,256,128]{2,1,0:T(8,128)(2,1)S(1)}, u32[]{:S(2)}, u32[]{:S(2)}) collective-permute-start(bf16[5,256,128]{2,1,0:T(8,128)(2,1)S(1)} %slice.58), channel_id=1, source_target_pairs={{0,2},{1,3},{2,4},{3,5},{4,6},{5,7},{6,8},{7,9},{8,10},{9,11},{10,... | collective-permute-start | bytes 983048 | tf_op jit(solution)/shard_map/ppermute | solution.py:246
  62.4 11.7 %collective-permute-start.4 = (bf16[5,256,128]{2,1,0:T(8,128)(2,1)S(1)}, bf16[5,256,128]{2,1,0:T(8,128)(2,1)S(1)}, u32[]{:S(2)}, u32[]{:S(2)}) collective-permute-start(bf16[5,256,128]{2,1,0:T(8,128)(2,1)S(1)} %slice.60), channel_id=1, source_target_pairs={{0,14},{1,15},{2,0},{3,1},{4,2},{5,3},{6,4},{7,5},{8,6},{9,7},{10,... | collective-permute-start | bytes 983048 | tf_op jit(solution)/shard_map/ppermute | solution.py:246
  72.1 8.8 %collective-permute-start.5 = (bf16[3,256,128]{2,1,0:T(8,128)(2,1)S(1)}, bf16[3,256,128]{2,1,0:T(8,128)(2,1)S(1)}, u32[]{:S(2)}, u32[]{:S(2)}) collective-permute-start(bf16[3,256,128]{2,1,0:T(8,128)(2,1)S(1)} %slice.62), channel_id=1, source_target_pairs={{0,2},{1,3},{2,4},{3,5},{4,6},{5,7},{6,8},{7,9},{8,10},{9,11},{10,... | collective-permute-start | bytes 589832 | tf_op jit(solution)/shard_map/ppermute | solution.py:246
  74.1 8.7 %collective-permute-start.6 = (bf16[3,256,128]{2,1,0:T(8,128)(2,1)S(1)}, bf16[3,256,128]{2,1,0:T(8,128)(2,1)S(1)}, u32[]{:S(2)}, u32[]{:S(2)}) collective-permute-start(bf16[3,256,128]{2,1,0:T(8,128)(2,1)S(1)} %slice.64), channel_id=1, source_target_pairs={{0,14},{1,15},{2,0},{3,1},{4,2},{5,3},{6,4},{7,5},{8,6},{9,7},{10,... | collective-permute-start | bytes 589832 | tf_op jit(solution)/shard_map/ppermute | solution.py:246
  80.9 8.5 %collective-permute-start.7 = (bf16[1,256,128]{2,1,0:T(8,128)(2,1)S(1)}, bf16[1,256,128]{2,1,0:T(8,128)(2,1)S(1)}, u32[]{:S(2)}, u32[]{:S(2)}) collective-permute-start(bf16[1,256,128]{2,1,0:T(8,128)(2,1)S(1)} %slice.66), channel_id=1, source_target_pairs={{0,2},{1,3},{2,4},{3,5},{4,6},{5,7},{6,8},{7,9},{8,10},{9,11},{10,... | collective-permute-start | bytes 196616 | tf_op jit(solution)/shard_map/ppermute | solution.py:246
  82.9 7.1 %collective-permute-start.8 = (bf16[1,256,128]{2,1,0:T(8,128)(2,1)S(1)}, bf16[1,256,128]{2,1,0:T(8,128)(2,1)S(1)}, u32[]{:S(2)}, u32[]{:S(2)}) collective-permute-start(bf16[1,256,128]{2,1,0:T(8,128)(2,1)S(1)} %slice.67), channel_id=1, source_target_pairs={{0,14},{1,15},{2,0},{3,1},{4,2},{5,3},{6,4},{7,5},{8,6},{9,7},{10,... | collective-permute-start | bytes 196616 | tf_op jit(solution)/shard_map/ppermute | solution.py:246
  90.6 6.7 %collective-permute-start.9 = (bf16[16,256,128]{2,1,0:T(8,128)(2,1)}, bf16[16,256,128]{2,1,0:T(8,128)(2,1)S(1)}, u32[]{:S(2)}, u32[]{:S(2)}) collective-permute-start(bf16[16,256,128]{2,1,0:T(8,128)(2,1)} %constant_dynamic-update-slice_fusion), channel_id=1, source_target_pairs={{0,1},{1,0},{2,3},{3,2},{4,5},{5,4},{6,7},{7,6},{8,9},{9,8},{10,11... | collective-permute-start | bytes 3145736 | tf_op jit(solution)/shard_map/ppermute | solution.py:249
  92.8 0.7 copy-start.5
  93.8 2.5 %copy-start.4 = (s32[2,768]{1,0:T(2,128)S(1)}, s32[2,768]{1,0:T(2,128)}, u32[]{:S(2)}) copy-start(s32[2,768]{1,0:T(2,128)} %param.10) | copy-start | bytes 18436
  93.9 3.5 %collective-permute-start = (bf16[32,20,128]{2,1,0:T(8,128)(2,1)S(1)}, bf16[32,20,128]{2,1,0:T(8,128)(2,1)S(1)}, u32[]{:S(2)}, u32[]{:S(2)}) collective-permute-start(bf16[32,20,128]{2,1,0:T(8,128)(2,1)S(1)} %slice.55), channel_id=1, source_target_pairs={{0,1},{1,0},{2,3},{3,2},{4,5},{5,4},{6,7},{7,6},{8,9},{9,8},{10,11... | collective-permute-start | bytes 491528 | tf_op jit(solution)/shard_map/ppermute | solution.py:249

commit v2 on v1

--- a/solution.py
+++ b/solution.py
@@ -22,43 +22,36 @@
 LIMIT = 48 * 1024 * 1024
 
 
-def split_cache(z, kv):
-    def kernel(z_ref, kv_ref, own_ref, right_ref, left_ref, sems):
-        me = z_ref[0]
-        copies = []
-
-        def send(side, dist, dst):
-            col = pl.multiple_of(lax.rem(me + dist, KVH) * HD, HD)
-            sem = sems.at[len(copies)]
-            copies.append(
-                pltpu.make_async_copy(kv_ref.at[side, :, pl.ds(col, HD)], dst, sem)
-            )
-
-        for side in range(2):
-            for dist in range(1, 4):
-                send(side, dist, right_ref.at[2 * (dist - 1) + side])
-                send(side, KVH - dist, left_ref.at[2 * (dist - 1) + side])
-            send(side, 0, own_ref.at[side])
-        send(0, 4, right_ref.at[6])
-        send(1, 4, left_ref.at[6])
-        for copy in copies:
-            copy.start()
-        for copy in copies:
-            copy.wait()
+def split_cache(ident, kv):
+    def kernel(id_ref, kv_ref, keep_ref, give_ref):
+        z, core = id_ref[0], id_ref[1]
+        step = 1 - 2 * core
+
+        def cut(side, dist):
+            col = pl.multiple_of(lax.rem(z + dist + KVH, KVH) * HD, HD)
+            return kv_ref[side, :, pl.ds(col, HD)]
+
+        for dist in range(1, 4):
+            for side in range(2):
+                keep_ref[2 * (dist - 1) + side] = cut(side, dist * step)
+                give_ref[2 * (dist - 1) + side] = cut(side, -dist * step)
+        keep_ref[6] = cut(core, 4)
+        give_ref[6] = cut(1 - core, 4)
+        give_ref[7] = cut(0, 0)
+        give_ref[8] = cut(1, 0)
 
     return pl.pallas_call(
         kernel,
         out_shape=(
-            jax.ShapeDtypeStruct((2, SPAN, HD), kv.dtype),
             jax.ShapeDtypeStruct((7, SPAN, HD), kv.dtype),
-            jax.ShapeDtypeStruct((7, SPAN, HD), kv.dtype),
+            jax.ShapeDtypeStruct((9, SPAN, HD), kv.dtype),
         ),
-        in_specs=[pl.BlockSpec(memory_space=SMEM), pl.BlockSpec(memory_space=pl.ANY)],
-        out_specs=[pl.BlockSpec(memory_space=pl.ANY)] * 3,
-        scratch_shapes=[pltpu.SemaphoreType.DMA((16,))],
+        in_specs=[pl.BlockSpec(memory_space=SMEM), pl.BlockSpec(memory_space=VMEM)],
+        out_specs=[pl.BlockSpec(memory_space=VMEM)] * 2,
+        compiler_params=pltpu.CompilerParams(vmem_limit_bytes=LIMIT),
         cost_estimate=pl.CostEstimate(flops=0, bytes_accessed=2 << 20, transcendentals=0),
         name="split_cache",
-    )(z, kv)
+    )(ident, kv)
 
 
 def pack_rows(pos, queries, new_kv):
@@ -95,30 +88,42 @@
     )(pos, queries, new_kv)
 
 
-def attend(info, received, new_sib, pieces, sib):
+def attend(info, received, new_sib, pieces):
     n_pieces = len(pieces)
-    layout = []
-    for i, dist in enumerate((0, -1, 1, -2, 2, -3, 3)):
-        layout += [(i, 0, 0, dist), (i, 1, 1, dist)]
-    layout += [(7, 0, 0, 4), (8, 0, 1, 4)]
 
     def kernel(info_ref, recv_ref, ns_ref, *refs):
         piece_refs = refs[:n_pieces]
-        sib_ref, out_ref, kbuf, vbuf, qs, kn, vn, sems = refs[n_pieces:]
+        out_ref, kvbuf, qs, kn, vn, sems = refs[n_pieces:]
         z, core = info_ref[5, 0], info_ref[5, 1]
+        step = 1 - 2 * core
         copies = []
-        for unit, (i, u, side, dist) in enumerate(layout):
-            src_z = lax.rem(z + dist + KVH, KVH)
-            for other in range(2):
-                owner = src_z * 2 + (core if other == 0 else 1 - core)
-                rows = pl.ds(pl.multiple_of(owner * SPAN, SPAN), SPAN)
-                src = piece_refs[i].at[u] if other == 0 else sib_ref.at[unit]
-                dst = (kbuf, vbuf)[side].at[rows]
-                copies.append(pltpu.make_async_copy(src, dst, sems.at[len(copies)]))
+
+        def place(piece, unit, side, src_z, src_core):
+            owner = lax.rem(src_z + KVH, KVH) * 2 + src_core
+            rows = pl.ds(pl.multiple_of(owner * SPAN, SPAN), SPAN)
+            copies.append(
+                pltpu.make_async_copy(
+                    piece_refs[piece].at[unit], kvbuf.at[side, rows], sems.at[len(copies)]
+                )
+            )
+
+        for side in range(2):
+            place(0, 7 + side, side, z, core)
+            place(1, 7 + side, side, z, 1 - core)
+            for dist in range(1, 4):
+                for half in range(2):
+                    unit = 2 * half + side
+                    there = core if half == 0 else 1 - core
+                    place(1 + dist, unit, side, z - step * dist, there)
+                    far, at = (6, 4 * (dist - 1)) if dist < 3 else (7, 0)
+                    place(far, at + unit, side, z + step * dist, 1 - there)
+        for half in range(2):
+            there = core if half == 0 else 1 - core
+            place(5, half, core, z + 4, there)
+            place(7, 4 + half, 1 - core, z + 4, 1 - there)
         for copy in copies:
             copy.start()
-        kbuf[KVH * 2 * SPAN :, :] = jnp.zeros((WIN, HD), jnp.bfloat16)
-        vbuf[KVH * 2 * SPAN :, :] = jnp.zeros((WIN, HD), jnp.bfloat16)
+        kvbuf[:, KVH * 2 * SPAN :, :] = jnp.zeros((2, WIN, HD), jnp.bfloat16)
         low_half = lax.broadcasted_iota(jnp.int32, (TOK, HD), 1) < HD // 2
         fill = jnp.zeros((16 - TOK, HD), jnp.float32)
         for j in range(RD):
@@ -158,7 +163,7 @@
                 start, length = info_ref[1, j], info_ref[2, j]
                 base = pl.multiple_of((start // 16) * 16, 16)
                 off = start - base
-                keys = jnp.concatenate([kbuf[pl.ds(base, WIN), :], kn[j]], axis=0)
+                keys = jnp.concatenate([kvbuf[0, pl.ds(base, WIN), :], kn[j]], axis=0)
                 sc = lax.dot_general(
                     qs[j], keys, (((1,), (1,)), ((), ())), preferred_element_type=jnp.float32
                 )
@@ -177,7 +182,7 @@
                 weights.append((jnp.concatenate([wc, wf], axis=1), total))
             for j, (w, total) in zip(js, weights):
                 base = pl.multiple_of((info_ref[1, j] // 16) * 16, 16)
-                vals = jnp.concatenate([vbuf[pl.ds(base, WIN), :], vn[j]], axis=0)
+                vals = jnp.concatenate([kvbuf[1, pl.ds(base, WIN), :], vn[j]], axis=0)
                 high = w.astype(jnp.bfloat16)
                 low = (w - high.astype(jnp.float32)).astype(jnp.bfloat16)
                 dims = (((1,), (0,)), ((), ()))
@@ -198,11 +203,10 @@
             pl.BlockSpec(memory_space=VMEM),
             pl.BlockSpec(memory_space=VMEM),
         ]
-        + [pl.BlockSpec(memory_space=pl.ANY)] * (n_pieces + 1),
+        + [pl.BlockSpec(memory_space=pl.ANY)] * n_pieces,
         out_specs=pl.BlockSpec(memory_space=VMEM),
         scratch_shapes=[
-            pltpu.VMEM((KVH * 2 * SPAN + WIN, HD), jnp.bfloat16),
-            pltpu.VMEM((KVH * 2 * SPAN + WIN, HD), jnp.bfloat16),
+            pltpu.VMEM((2, KVH * 2 * SPAN + WIN, HD), jnp.bfloat16),
             pltpu.VMEM((RD, QR, HD), jnp.bfloat16),
             pltpu.VMEM((RD, 16, HD), jnp.bfloat16),
             pltpu.VMEM((RD, 16, HD), jnp.bfloat16),
@@ -213,7 +217,7 @@
             flops=24 * 40 * 400 * 128 * 6, bytes_accessed=4 << 20, transcendentals=24 * 40 * 400
         ),
         name="attend",
-    )(info, received, new_sib, *pieces, sib)
+    )(info, received, new_sib, *pieces)
 
 
 def unpack_rows(pos, received):
@@ -242,18 +246,21 @@
     n_dp = lax.axis_size("dp")
 
     def along_z(x, k):
-        perm = [(t, (t // 2 + k) % KVH * 2 + t % 2) for t in range(16)]
+        perm = [(t, (t // 2 + (k if t % 2 == 0 else -k)) % KVH * 2 + t % 2) for t in range(16)]
         return lax.ppermute(x, "tensor", perm)
 
     def sibling(x):
         return lax.ppermute(x, "tensor", [(t, t ^ 1) for t in range(16)])
 
-    own, right, left = split_cache(z.reshape(1).astype(jnp.int32), kv_cache)
-    pieces = [own]
-    for _ in range(4):
-        right, left = along_z(right, 1), along_z(left, -1)
-        pieces += [right[:2], left[:2]]
-        right, left = right[2:], left[2:]
+    keep, give = split_cache(jnp.stack([z, core]).astype(jnp.int32), kv_cache)
+    got = sibling(give)
+    moved = []
+    for k in range(1, 5):
+        cut = slice(2 * k - 2, min(2 * k, 7))
+        moved.append(along_z(jnp.concatenate([keep[cut], got[cut]], axis=0), k))
+    crossed_a = sibling(jnp.concatenate(moved[:2], axis=0))
+    crossed_b = sibling(jnp.concatenate(moved[2:], axis=0))
+    pieces = [give, got] + moved + [crossed_a, crossed_b]
 
     group_of = dest // RD
     mine = lax.dynamic_slice_in_dim(group_of, me_dp * RD, RD)
@@ -274,8 +281,7 @@
     packed = pack_rows(send_pos, queries, new_kv)
     received = lax.all_to_all(packed, "dp", split_axis=0, concat_axis=0, tiled=True)
     new_sib = sibling(received[:, 2 * QR :])
-    sib = sibling(jnp.concatenate(pieces, axis=0))
-    outs = attend(info, received, new_sib, pieces, sib)
+    outs = attend(info, received, new_sib, pieces)
     back = lax.all_to_all(
         outs.reshape(n_dp, 2 * QR, HD), "dp", split_axis=0, concat_axis=0, tiled=True
     )

time: 136 us -> 101 us (0.74)
  the two profiles are of different devices: /device:TPU:2 before, /device:TPU:64 now
where the time goes in v2:
time: 101 us; the launch traced here: 100 us
  starting transfers between devices  37 us (37%)
  blocking collectives  30.5 us (30%)
  waiting for transfers between devices  15.6 us (15%)
  Pallas kernels  10.5 us (10%)
  other arithmetic  3.51 us (3%)
  local copies, waits for them, and re-layouts  3.05 us (3%)
    all_to_all x1, blocking collectives, body(): lax.all_to_all(outs.reshape(n_dp, 2 * QR, HD), 'dp', split_axis=0, concat...  30.5 us
    ppermute x4, starting transfers between devices, along_z(): return lax.ppermute(x, 'tensor', perm)  18.7 us
    ppermute x4, waiting for transfers between devices, along_z(): return lax.ppermute(x, 'tensor', perm)  12.8 us
    all_to_all x1, starting transfers between devices, body(): lax.all_to_all(packed, 'dp', split_axis=0, concat_axis=0, tiled=True)  10.1 us
    ppermute x4, starting transfers between devices, sibling(): return lax.ppermute(x, 'tensor', [(t, t ^ 1) for t in range(16)])  8.27 us
    pallas_call x1, Pallas kernels, attend(): pl.pallas_call(kernel, out_shape=jax.ShapeDtypeStruct((64, QR, HD), jnp.b...  7.34 us
    ppermute x4, waiting for transfers between devices, sibling(): return lax.ppermute(x, 'tensor', [(t, t ^ 1) for t in range(16)])  2.73 us
  transfers between devices with their start and end apart: 9, of which 5 were waited for; matrix products, arithmetic and copies ran while one was open for 4% of the time, Pallas kernels for 1%

profile of v2, /device:TPU:64, one launch (start us, length us, event | category | flops | bytes accessed | tf_op | source)
XLA Modules:
  0.0 100.5 jit_solution(15784767081663468649)
XLA Ops:
  0.0 0.7 broadcast_compare_fusion.1
  0.7 0.1 dynamic_slice.3
  0.8 0.2 convert_reduce_fusion.1
  1.0 0.1 multiply_add_fusion.pos_ref
  1.1 0.9 copy.16.n_ref
  2.0 0.0 copy-done.1
  2.0 0.1 copy.15.q_ref
  2.1 1.7 %pack_rows.1 = bf16[32,100,128]{2,1,0:T(8,128)(2,1)} custom-call(s32[24]{0:T(128)S(1)} %multiply_add_fusion.pos_ref, bf16[2,24,5,512]{3,2,1,0:T(8,128)(2,1)S(1)} %copy.15.q_ref, bf16[2,2,24,5,64]{4,3,2,1,0:T(8,128)(2,1)S(1)} %copy.16.n_ref), custom_call_target="tpu_custom_call" | custom-call | bytes 2097152 | tf_op jit(solution)/shard_map/pack_rows/pallas_call | solution.py:72
  3.8 10.1 %all-to-all-start = ((bf16[32,100,128]{2,1,0:T(8,128)(2,1)}), bf16[32,100,128]{2,1,0:T(8,128)(2,1)S(1)}, u32[]{:S(2)}, u32[]{:S(2)}) async-start(bf16[32,100,128]{2,1,0:T(8,128)(2,1)} %pack_rows.1), calls=%async_computation | async-start | bytes 1703936 | tf_op jit(solution)/shard_map/all_to_all | solution.py:282
  13.9 0.1 pad_add_fusion.id_ref
  14.0 0.0 copy-done
  14.0 0.8 split_cache.1
  14.8 1.9 %collective-permute-start.1 = (bf16[9,256,128]{2,1,0:T(8,128)(2,1)S(1)}, bf16[9,256,128]{2,1,0:T(8,128)(2,1)S(1)}, u32[]{:S(2)}, u32[]{:S(2)}) collective-permute-start(bf16[9,256,128]{2,1,0:T(8,128)(2,1)S(1)} %get-tuple-element.7.refs_0_), channel_id=1, source_target_pairs={{0,1},{1,0},{2,3},{3,2},{4,5},{5,4},{6,7},{7,6},{8,9},{9,8},{10,11... | collective-permute-start | bytes 1769480 | tf_op jit(solution)/shard_map/ppermute | solution.py:253
  16.8 0.1 and.36
  16.9 0.1 copy.13
  17.0 0.2 convert_reduce_fusion
  17.2 1.5 %collective-permute-done.1.refs_1_ = bf16[9,256,128]{2,1,0:T(8,128)(2,1)S(1)} collective-permute-done((bf16[9,256,128]{2,1,0:T(8,128)(2,1)S(1)}, bf16[9,256,128]{2,1,0:T(8,128)(2,1)S(1)}, u32[]{:S(2)}, u32[]{:S(2)}) %collective-permute-start.1) | collective-permute-done | bytes 589856 | tf_op jit(solution)/shard_map/ppermute | solution.py:253
  18.7 10.0 %collective-permute-start.5 = (bf16[2,256,128]{2,1,0:T(8,128)(2,1)S(1)}, bf16[2,256,128]{2,1,0:T(8,128)(2,1)S(1)}, u32[]{:S(2)}, u32[]{:S(2)}) collective-permute-start(bf16[2,256,128]{2,1,0:T(8,128)(2,1)S(1)} %pad_maximum_fusion.5), channel_id=1, source_target_pairs={{0,8},{1,9},{2,10},{3,11},{4,12},{5,13},{6,14},{7,15},{8,0},{9,1},... | collective-permute-start | bytes 393224 | tf_op jit(solution)/shard_map/ppermute | solution.py:250
  28.8 3.4 %collective-permute-start.2 = (bf16[4,256,128]{2,1,0:T(8,128)(2,1)S(1)}, bf16[4,256,128]{2,1,0:T(8,128)(2,1)S(1)}, u32[]{:S(2)}, u32[]{:S(2)}) collective-permute-start(bf16[4,256,128]{2,1,0:T(8,128)(2,1)S(1)} %pad_maximum_fusion.2), channel_id=1, source_target_pairs={{0,2},{1,15},{2,4},{3,1},{4,6},{5,3},{6,8},{7,5},{8,10},{9,7},{10,... | collective-permute-start | bytes 786440 | tf_op jit(solution)/shard_map/ppermute | solution.py:250
  32.3 2.8 %collective-permute-start.3 = (bf16[4,256,128]{2,1,0:T(8,128)(2,1)S(1)}, bf16[4,256,128]{2,1,0:T(8,128)(2,1)S(1)}, u32[]{:S(2)}, u32[]{:S(2)}) collective-permute-start(bf16[4,256,128]{2,1,0:T(8,128)(2,1)S(1)} %pad_maximum_fusion.3), channel_id=1, source_target_pairs={{0,4},{1,13},{2,6},{3,15},{4,8},{5,1},{6,10},{7,3},{8,12},{9,5},{1... | collective-permute-start | bytes 786440 | tf_op jit(solution)/shard_map/ppermute | solution.py:250
  35.1 0.0 copy-start.2
  35.2 2.5 %collective-permute-start.4 = (bf16[4,256,128]{2,1,0:T(8,128)(2,1)S(1)}, bf16[4,256,128]{2,1,0:T(8,128)(2,1)S(1)}, u32[]{:S(2)}, u32[]{:S(2)}) collective-permute-start(bf16[4,256,128]{2,1,0:T(8,128)(2,1)S(1)} %pad_maximum_fusion.4), channel_id=1, source_target_pairs={{0,6},{1,11},{2,8},{3,13},{4,10},{5,15},{6,12},{7,1},{8,14},{9,3},... | collective-permute-start | bytes 786440 | tf_op jit(solution)/shard_map/ppermute | solution.py:250
  37.6 0.0 copy-done.2
  37.6 0.1 broadcast_compare_fusion
  37.7 0.7 collective-permute-done.2.refs_2_
  38.4 7.2 %collective-permute-done.3.refs_3_ = bf16[4,256,128]{2,1,0:T(8,128)(2,1)S(1)} collective-permute-done((bf16[4,256,128]{2,1,0:T(8,128)(2,1)S(1)}, bf16[4,256,128]{2,1,0:T(8,128)(2,1)S(1)}, u32[]{:S(2)}, u32[]{:S(2)}) %collective-permute-start.3) | collective-permute-done | bytes 262176 | tf_op jit(solution)/shard_map/ppermute | solution.py:250
  45.6 0.9 pad_maximum_fusion
  46.5 1.9 %collective-permute-start.6 = (bf16[8,256,128]{2,1,0:T(8,128)(2,1)}, bf16[8,256,128]{2,1,0:T(8,128)(2,1)S(1)}, u32[]{:S(2)}, u32[]{:S(2)}) collective-permute-start(bf16[8,256,128]{2,1,0:T(8,128)(2,1)} %pad_maximum_fusion), channel_id=1, source_target_pairs={{0,1},{1,0},{2,3},{3,2},{4,5},{5,4},{6,7},{7,6},{8,9},{9,8},{10,11... | collective-permute-start | bytes 1572872 | tf_op jit(solution)/shard_map/ppermute | solution.py:253
  48.4 0.0 collective-permute-done.5.refs_5_
  48.4 4.9 %collective-permute-done.4.refs_4_ = bf16[4,256,128]{2,1,0:T(8,128)(2,1)S(1)} collective-permute-done((bf16[4,256,128]{2,1,0:T(8,128)(2,1)S(1)}, bf16[4,256,128]{2,1,0:T(8,128)(2,1)S(1)}, u32[]{:S(2)}, u32[]{:S(2)}) %collective-permute-start.4) | collective-permute-done | bytes 262176 | tf_op jit(solution)/shard_map/ppermute | solution.py:250
  53.3 0.8 pad_maximum_fusion.1
  54.1 2.0 %collective-permute-start.7 = (bf16[6,256,128]{2,1,0:T(8,128)(2,1)}, bf16[6,256,128]{2,1,0:T(8,128)(2,1)}, u32[]{:S(2)}, u32[]{:S(2)}) collective-permute-start(bf16[6,256,128]{2,1,0:T(8,128)(2,1)} %pad_maximum_fusion.1), channel_id=1, source_target_pairs={{0,1},{1,0},{2,3},{3,2},{4,5},{5,4},{6,7},{7,6},{8,9},{9,8},{10,11... | collective-permute-start | bytes 1179656 | tf_op jit(solution)/shard_map/ppermute | solution.py:253
  56.2 0.1 select_reduce_fusion.2
  56.3 0.1 copy.14
  56.4 0.1 add.43
  56.5 0.2 select_reduce_fusion.1
  56.7 0.0 all-to-all-done.recv_ref
  56.7 0.0 copy-start.3
  56.7 0.7 slice.39
  57.4 2.4 %collective-permute-start = (bf16[32,20,128]{2,1,0:T(8,128)(2,1)}, bf16[32,20,128]{2,1,0:T(8,128)(2,1)}, u32[]{:S(2)}, u32[]{:S(2)}) collective-permute-start(bf16[32,20,128]{2,1,0:T(8,128)(2,1)} %slice.39), channel_id=1, source_target_pairs={{0,1},{1,0},{2,3},{3,2},{4,5},{5,4},{6,7},{7,6},{8,9},{9,8},{10,11... | collective-permute-start | bytes 491528 | tf_op jit(solution)/shard_map/ppermute | solution.py:253
  59.8 0.1 select_reduce_fusion
  60.0 0.0 collective-permute-done.7.refs_7_
  60.0 0.0 collective-permute-done.6.refs_6_
  60.0 1.2 %collective-permute-done.ns_ref = bf16[32,20,128]{2,1,0:T(8,128)(2,1)} collective-permute-done((bf16[32,20,128]{2,1,0:T(8,128)(2,1)}, bf16[32,20,128]{2,1,0:T(8,128)(2,1)}, u32[]{:S(2)}, u32[]{:S(2)}) %collective-permute-start) | collective-permute-done | bytes 163872 | tf_op jit(solution)/shard_map/ppermute | solution.py:253
  61.2 7.3 %attend.1 = bf16[64,40,128]{2,1,0:T(8,128)(2,1)S(1)} custom-call(s32[6,24]{1,0:T(8,128)S(1)} %stack.21.info_ref, bf16[32,100,128]{2,1,0:T(8,128)(2,1)S(1)} %all-to-all-done.recv_ref, bf16[32,20,128]{2,1,0:T(8,128)(2,1)} %collective-permute-done.ns_ref, bf16[9,256,128]{2,1,0:T(8,128)(2,1)S(1)} %get-tuple-element.7.refs_0_, ...), custom_call_target="tpu_custom_call" | custom-call | flops 294912000 | bytes 4194304 | tf_op jit(solution)/shard_map/attend/pallas_call | solution.py:198
  68.5 30.5 %all_to_all.10 = bf16[32,80,128]{2,1,0:T(8,128)(2,1)S(1)} all-to-all(bf16[32,80,128]{2,1,0:T(8,128)(2,1)S(1)} %bitcast.8), channel_id=1, replica_groups=mesh['dp'=32,'tensor'=16] {'dp'}, dimensions={0} | all-to-all | bytes 1310720 | tf_op jit(solution)/shard_map/all_to_all | solution.py:285
  99.0 0.7 unpack_rows.1
  99.7 0.8 copy.17
  (19 shorter events, 0.2 us)
Async XLA Ops:
  0.0 2.0 %copy-start.1 = (bf16[2,24,5,512]{3,1,2,0:T(8,128)(2,1)S(1)}, bf16[2,24,5,512]{3,1,2,0:T(8,128)(2,1)}, u32[]{:S(2)}) copy-start(bf16[2,24,5,512]{3,1,2,0:T(8,128)(2,1)} %param.6) | copy-start | bytes 737284
  3.8 10.2 %copy-start = (bf16[2,256,1024]{2,1,0:T(8,128)(2,1)S(1)}, bf16[2,256,1024]{2,1,0:T(8,128)(2,1)}, u32[]{:S(2)}) copy-start(bf16[2,256,1024]{2,1,0:T(8,128)(2,1)} %kv_ref.1) | copy-start | bytes 3145732
  3.8 52.9 %all-to-all-start = ((bf16[32,100,128]{2,1,0:T(8,128)(2,1)}), bf16[32,100,128]{2,1,0:T(8,128)(2,1)S(1)}, u32[]{:S(2)}, u32[]{:S(2)}) async-start(bf16[32,100,128]{2,1,0:T(8,128)(2,1)} %pack_rows.1), calls=%async_computation | async-start | bytes 1703936 | tf_op jit(solution)/shard_map/all_to_all | solution.py:282
  14.8 3.9 %collective-permute-start.1 = (bf16[9,256,128]{2,1,0:T(8,128)(2,1)S(1)}, bf16[9,256,128]{2,1,0:T(8,128)(2,1)S(1)}, u32[]{:S(2)}, u32[]{:S(2)}) collective-permute-start(bf16[9,256,128]{2,1,0:T(8,128)(2,1)S(1)} %get-tuple-element.7.refs_0_), channel_id=1, source_target_pairs={{0,1},{1,0},{2,3},{3,2},{4,5},{5,4},{6,7},{7,6},{8,9},{9,8},{10,11... | collective-permute-start | bytes 1769480 | tf_op jit(solution)/shard_map/ppermute | solution.py:253
  18.7 29.7 %collective-permute-start.5 = (bf16[2,256,128]{2,1,0:T(8,128)(2,1)S(1)}, bf16[2,256,128]{2,1,0:T(8,128)(2,1)S(1)}, u32[]{:S(2)}, u32[]{:S(2)}) collective-permute-start(bf16[2,256,128]{2,1,0:T(8,128)(2,1)S(1)} %pad_maximum_fusion.5), channel_id=1, source_target_pairs={{0,8},{1,9},{2,10},{3,11},{4,12},{5,13},{6,14},{7,15},{8,0},{9,1},... | collective-permute-start | bytes 393224 | tf_op jit(solution)/shard_map/ppermute | solution.py:250
  28.8 9.6 %collective-permute-start.2 = (bf16[4,256,128]{2,1,0:T(8,128)(2,1)S(1)}, bf16[4,256,128]{2,1,0:T(8,128)(2,1)S(1)}, u32[]{:S(2)}, u32[]{:S(2)}) collective-permute-start(bf16[4,256,128]{2,1,0:T(8,128)(2,1)S(1)} %pad_maximum_fusion.2), channel_id=1, source_target_pairs={{0,2},{1,15},{2,4},{3,1},{4,6},{5,3},{6,8},{7,5},{8,10},{9,7},{10,... | collective-permute-start | bytes 786440 | tf_op jit(solution)/shard_map/ppermute | solution.py:250
  32.3 13.4 %collective-permute-start.3 = (bf16[4,256,128]{2,1,0:T(8,128)(2,1)S(1)}, bf16[4,256,128]{2,1,0:T(8,128)(2,1)S(1)}, u32[]{:S(2)}, u32[]{:S(2)}) collective-permute-start(bf16[4,256,128]{2,1,0:T(8,128)(2,1)S(1)} %pad_maximum_fusion.3), channel_id=1, source_target_pairs={{0,4},{1,13},{2,6},{3,15},{4,8},{5,1},{6,10},{7,3},{8,12},{9,5},{1... | collective-permute-start | bytes 786440 | tf_op jit(solution)/shard_map/ppermute | solution.py:250
  35.1 2.5 %copy-start.2 = (s32[768]{0:T(1024)S(1)}, s32[768]{0:T(1024)}, u32[]{:S(2)}) copy-start(s32[768]{0:T(1024)} %param.11) | copy-start | bytes 9220
  35.2 18.2 %collective-permute-start.4 = (bf16[4,256,128]{2,1,0:T(8,128)(2,1)S(1)}, bf16[4,256,128]{2,1,0:T(8,128)(2,1)S(1)}, u32[]{:S(2)}, u32[]{:S(2)}) collective-permute-start(bf16[4,256,128]{2,1,0:T(8,128)(2,1)S(1)} %pad_maximum_fusion.4), channel_id=1, source_target_pairs={{0,6},{1,11},{2,8},{3,13},{4,10},{5,15},{6,12},{7,1},{8,14},{9,3},... | collective-permute-start | bytes 786440 | tf_op jit(solution)/shard_map/ppermute | solution.py:250
  46.5 13.5 %collective-permute-start.6 = (bf16[8,256,128]{2,1,0:T(8,128)(2,1)}, bf16[8,256,128]{2,1,0:T(8,128)(2,1)S(1)}, u32[]{:S(2)}, u32[]{:S(2)}) collective-permute-start(bf16[8,256,128]{2,1,0:T(8,128)(2,1)} %pad_maximum_fusion), channel_id=1, source_target_pairs={{0,1},{1,0},{2,3},{3,2},{4,5},{5,4},{6,7},{7,6},{8,9},{9,8},{10,11... | collective-permute-start | bytes 1572872 | tf_op jit(solution)/shard_map/ppermute | solution.py:253
  54.1 2.1 %copy-start.4 = (s32[1,24]{1,0:T(1,128)S(1)}, s32[1,24]{1,0:T(1,128)}, u32[]{:S(2)}) copy-start(s32[1,24]{1,0:T(1,128)} %param.9) | copy-start | bytes 292
  54.1 5.8 %collective-permute-start.7 = (bf16[6,256,128]{2,1,0:T(8,128)(2,1)}, bf16[6,256,128]{2,1,0:T(8,128)(2,1)}, u32[]{:S(2)}, u32[]{:S(2)}) collective-permute-start(bf16[6,256,128]{2,1,0:T(8,128)(2,1)} %pad_maximum_fusion.1), channel_id=1, source_target_pairs={{0,1},{1,0},{2,3},{3,2},{4,5},{5,4},{6,7},{7,6},{8,9},{9,8},{10,11... | collective-permute-start | bytes 1179656 | tf_op jit(solution)/shard_map/ppermute | solution.py:253
  56.7 3.1 %copy-start.3 = (s32[2,768]{1,0:T(2,128)S(1)}, s32[2,768]{1,0:T(2,128)}, u32[]{:S(2)}) copy-start(s32[2,768]{1,0:T(2,128)} %param.10) | copy-start | bytes 18436
  57.4 3.8 %collective-permute-start = (bf16[32,20,128]{2,1,0:T(8,128)(2,1)}, bf16[32,20,128]{2,1,0:T(8,128)(2,1)}, u32[]{:S(2)}, u32[]{:S(2)}) collective-permute-start(bf16[32,20,128]{2,1,0:T(8,128)(2,1)} %slice.39), channel_id=1, source_target_pairs={{0,1},{1,0},{2,3},{3,2},{4,5},{5,4},{6,7},{7,6},{8,9},{9,8},{10,11... | collective-permute-start | bytes 491528 | tf_op jit(solution)/shard_map/ppermute | solution.py:253

commit v3 on v2

v3 whole, which is shorter than its diff:
```python
import jax
import jax.numpy as jnp
from jax import lax
from jax.experimental import pallas as pl
from jax.experimental.pallas import tpu as pltpu
from jax.sharding import PartitionSpec as P

HQ = 64
KVH = 8
HD = 128
CH = 5
STEPS = 2
RD = 24
SPAN = 256
WIN = 384
TOK = STEPS * CH
PER = 4
QR = PER * TOK
SCALE = HD**-0.5
VMEM = pltpu.MemorySpace.VMEM
SMEM = pltpu.MemorySpace.SMEM
LIMIT = 48 * 1024 * 1024


def split_cache(ident, kv):
    def kernel(id_ref, kv_ref, keep_ref, give_ref, sems):
        z, core = id_ref[0], id_ref[1]
        step = 1 - 2 * core
        copies = []

        def put(ref, unit, side, dist):
            col = pl.multiple_of(lax.rem(z + dist + KVH, KVH) * HD, HD)
            src = kv_ref.at[side, :, pl.ds(col, HD)]
            dst = ref.at[pl.ds(unit * SPAN, SPAN)]
            copies.append(pltpu.make_async_copy(src, dst, sems.at[len(copies)]))

        for dist in range(1, 4):
            for side in range(2):
                put(give_ref, 2 * (dist - 1) + side, side, -dist * step)
                put(keep_ref, 2 * (dist - 1) + side, side, dist * step)
        put(give_ref, 6, 1 - core, 4)
        put(keep_ref, 6, core, 4)
        put(give_ref, 7, 0, 0)
        put(give_ref, 8, 1, 0)
        for copy in copies:
            copy.start()
        for copy in copies:
            copy.wait()

    return pl.pallas_call(
        kernel,
        out_shape=(
            jax.ShapeDtypeStruct((7 * SPAN, HD), kv.dtype),
            jax.ShapeDtypeStruct((9 * SPAN, HD), kv.dtype),
        ),
        in_specs=[pl.BlockSpec(memory_space=SMEM), pl.BlockSpec(memory_space=pl.ANY)],
        out_specs=[pl.BlockSpec(memory_space=VMEM)] * 2,
        scratch_shapes=[pltpu.SemaphoreType.DMA((16,))],
        compiler_params=pltpu.CompilerParams(vmem_limit_bytes=LIMIT),
        cost_estimate=pl.CostEstimate(flops=0, bytes_accessed=2 << 20, transcendentals=0),
        name="split_cache",
    )(ident, kv)


def join_cores(keep, got):
    sizes = [4, 4, 4, 2]

    def kernel(keep_ref, got_ref, *outs):
        for i, out in enumerate(outs):
            rows = sizes[i] // 2 * SPAN
            out[:rows, :] = keep_ref[2 * i * SPAN : 2 * i * SPAN + rows, :]
            out[rows:, :] = got_ref[2 * i * SPAN : 2 * i * SPAN + rows, :]

    return pl.pallas_call(
        kernel,
        out_shape=[jax.ShapeDtypeStruct((n * SPAN, HD), keep.dtype) for n in sizes],
        in_specs=[pl.BlockSpec(memory_space=VMEM)] * 2,
        out_specs=[pl.BlockSpec(memory_space=VMEM)] * 4,
        compiler_params=pltpu.CompilerParams(vmem_limit_bytes=LIMIT),
        cost_estimate=pl.CostEstimate(flops=0, bytes_accessed=2 << 20, transcendentals=0),
        name="join_cores",
    )(keep, got)


def pack_rows(dest, first, queries, new_kv):
    def kernel(dest_ref, first_ref, q_ref, n_ref, out_ref, pos_ref, seen, qf, nf, qs, ns):
        for g in range(32):
            seen[g] = 0
        for j in range(RD):
            g = dest_ref[first_ref[0] + j] // RD
            pos_ref[j] = 2 * g + seen[g]
            seen[g] = 1
        for s in range(STEPS):
            for c in range(CH):
                row = (s * CH + c) * RD
                q = q_ref[s, c].astype(jnp.float32)
                for h in range(PER):
                    qf[h, row : row + RD, :] = q[:, h * HD : (h + 1) * HD]
                n = [n_ref[side, s, c].astype(jnp.float32) for side in range(2)]
                nf[row : row + RD, :] = jnp.concatenate(n, axis=1)
        for j in range(RD):
            at = pos_ref[j]
            for s in range(STEPS):
                rows = pl.ds(s * CH * RD + j, CH, stride=RD)
                for h in range(PER):
                    row = h * TOK + s * CH
                    qs[at, row : row + CH, :] = qf[h, rows, :]
                ns[at, s * CH : (s + 1) * CH, :] = nf[rows, :]
        for g in range(32):
            block = [qs[2 * g], qs[2 * g + 1], ns[2 * g], ns[2 * g + 1]]
            out_ref[g] = jnp.concatenate(block, axis=0).astype(jnp.bfloat16)

    return pl.pallas_call(
        kernel,
        out_shape=(
            jax.ShapeDtypeStruct((32, 2 * (QR + TOK), HD), jnp.bfloat16),
            jax.ShapeDtypeStruct((RD,), jnp.int32),
        ),
        in_specs=[
            pl.BlockSpec(memory_space=SMEM),
            pl.BlockSpec(memory_space=SMEM),
            pl.BlockSpec(memory_space=VMEM),
            pl.BlockSpec(memory_space=VMEM),
        ],
        out_specs=(pl.BlockSpec(memory_space=VMEM), pl.BlockSpec(memory_space=SMEM)),
        scratch_shapes=[
            pltpu.SMEM((32,), jnp.int32),
            pltpu.VMEM((PER, TOK * RD, HD), jnp.float32),
            pltpu.VMEM((TOK * RD, HD), jnp.float32),
            pltpu.VMEM((64, QR, HD), jnp.float32),
            pltpu.VMEM((64, TOK, HD), jnp.float32),
        ],
        compiler_params=pltpu.CompilerParams(vmem_limit_bytes=LIMIT),
        cost_estimate=pl.CostEstimate(flops=0, bytes_accessed=2 << 20, transcendentals=0),
        name="pack_rows",
    )(dest, first, queries, new_kv)


def pick_rows(info, received):
    def kernel(info_ref, recv_ref, q_ref, n_ref):
        fill = jnp.zeros((16 - TOK, HD), jnp.float32)
        base = 2 * QR
        for j in range(RD):
            at = info_ref[0, j]
            g, second = at // 2, lax.rem(at, 2) == 1
            block = recv_ref[g].astype(jnp.float32)
            q_ref[j] = jnp.where(second, block[QR : 2 * QR], block[:QR]).astype(jnp.bfloat16)
            fresh = jnp.where(second, block[base + TOK :], block[base : base + TOK])
            n_ref[16 * j : 16 * j + 16, :] = jnp.concatenate([fresh, fill], axis=0).astype(
                jnp.bfloat16
            )

    return pl.pallas_call(
        kernel,
        out_shape=(
            jax.ShapeDtypeStruct((RD, QR, HD), jnp.bfloat16),
            jax.ShapeDtypeStruct((RD * 16, HD), jnp.bfloat16),
        ),
        in_specs=[pl.BlockSpec(memory_space=SMEM), pl.BlockSpec(memory_space=VMEM)],
        out_specs=[pl.BlockSpec(memory_space=VMEM)] * 2,
        compiler_params=pltpu.CompilerParams(vmem_limit_bytes=LIMIT),
        cost_estimate=pl.CostEstimate(flops=0, bytes_accessed=1 << 20, transcendentals=0),
        name="pick_rows",
    )(info, received)


def attend(info, queries, fresh, pieces):
    n_pieces = len(pieces)

    def kernel(info_ref, qs, fresh_ref, *refs):
        piece_refs = refs[:n_pieces]
        out_ref, kvbuf, kn, vn = refs[n_pieces:]
        z, core = info_ref[5, 0], info_ref[5, 1]
        step = 1 - 2 * core
        def place(piece, unit, side, src_z, src_core):
            owner = lax.rem(src_z + KVH, KVH) * 2 + src_core
            rows = pl.ds(pl.multiple_of(owner * SPAN, SPAN), SPAN)
            kvbuf[side, rows, :] = piece_refs[piece][unit * SPAN : (unit + 1) * SPAN, :]

        for side in range(2):
            place(0, 7 + side, side, z, core)
            place(1, 7 + side, side, z, 1 - core)
            for dist in range(1, 4):
                for half in range(2):
                    unit = 2 * half + side
                    there = core if half == 0 else 1 - core
                    place(1 + dist, unit, side, z - step * dist, there)
                    far, at = (6, 4 * (dist - 1)) if dist < 3 else (7, 0)
                    place(far, at + unit, side, z + step * dist, 1 - there)
        for half in range(2):
            there = core if half == 0 else 1 - core
            place(5, half, core, z + 4, there)
            place(7, 4 + half, 1 - core, z + 4, 1 - there)
        kvbuf[:, KVH * 2 * SPAN :, :] = jnp.zeros((2, WIN, HD), jnp.bfloat16)
        col = lax.broadcasted_iota(jnp.int32, (QR, WIN), 1)
        ncol = lax.broadcasted_iota(jnp.int32, (QR, 16), 1)
        nrow = lax.rem(lax.broadcasted_iota(jnp.int32, (QR, 16), 0), TOK)
        step_k, step_q = ncol // CH, nrow // CH
        pos_k, pos_q = lax.rem(ncol, CH), lax.rem(nrow, CH)
        need = jnp.where((step_k == step_q) & (pos_k <= pos_q), -1, 100)
        need = jnp.where(step_k < step_q, pos_k, need)
        need = jnp.where(ncol < TOK, need, 100)
        trow = lax.rem(lax.broadcasted_iota(jnp.int32, (QR, HD), 0), TOK)
        tstep, tpos = trow // CH, lax.rem(trow, CH)
        mine, theirs = fresh_ref[...].astype(jnp.float32), piece_refs[7][6 * SPAN :, :].astype(jnp.float32)
        low_half = lax.broadcasted_iota(jnp.int32, (RD * 16, HD), 1) < HD // 2
        low = jnp.where(core == 0, mine, theirs)
        high = jnp.where(core == 0, theirs, mine)
        kn[...] = jnp.where(low_half, low, pltpu.roll(high, HD // 2, 1)).astype(jnp.bfloat16)
        vn[...] = jnp.where(low_half, pltpu.roll(low, HD // 2, 1), high).astype(jnp.bfloat16)

        group = 12

        def some(it, carry):
            js = [it * group + i for i in range(group)]
            scores, values = [], []
            for j in js:
                start, length = info_ref[1, j], info_ref[2, j]
                base = pl.multiple_of((start // 16) * 16, 16)
                off = start - base
                keys = jnp.concatenate([kvbuf[0, pl.ds(base, WIN), :], kn[pl.ds(16 * j, 16), :]], axis=0)
                sc = lax.dot_general(
                    qs[j], keys, (((1,), (1,)), ((), ())), preferred_element_type=jnp.float32
                )
                cached = jnp.where(
                    (col >= off) & (col < off + length), sc[:, :WIN] * SCALE, -1e30
                )
                fresh = jnp.where(need <= info_ref[3, j], sc[:, WIN:] * SCALE, -1e30)
                scores.append((cached, fresh))
            weights = []
            for cached, fresh in scores:
                top = jnp.maximum(
                    jnp.max(cached, axis=1, keepdims=True), jnp.max(fresh, axis=1, keepdims=True)
                )
                wc, wf = jnp.exp(cached - top), jnp.exp(fresh - top)
                total = jnp.sum(wc, axis=1, keepdims=True) + jnp.sum(wf, axis=1, keepdims=True)
                weights.append((jnp.concatenate([wc, wf], axis=1), total))
            for j, (w, total) in zip(js, weights):
                base = pl.multiple_of((info_ref[1, j] // 16) * 16, 16)
                vals = jnp.concatenate([kvbuf[1, pl.ds(base, WIN), :], vn[pl.ds(16 * j, 16), :]], axis=0)
                high = w.astype(jnp.bfloat16)
                low = (w - high.astype(jnp.float32)).astype(jnp.bfloat16)
                dims = (((1,), (0,)), ((), ()))
                acc = lax.dot_general(high, vals, dims, preferred_element_type=jnp.float32)
                acc += lax.dot_general(low, vals, dims, preferred_element_type=jnp.float32)
                limit = jnp.where(tstep == 0, info_ref[3, j], info_ref[4, j])
                out = jnp.where(tpos <= limit, acc / total, 0.0)
                out_ref[info_ref[0, j]] = out.astype(jnp.bfloat16)
            return carry

        lax.fori_loop(0, RD // group, some, 0)

    return pl.pallas_call(
        kernel,
        out_shape=jax.ShapeDtypeStruct((64, QR, HD), jnp.bfloat16),
        in_specs=[
            pl.BlockSpec(memory_space=SMEM),
            pl.BlockSpec(memory_space=VMEM),
            pl.BlockSpec(memory_space=VMEM),
        ]
        + [pl.BlockSpec(memory_space=VMEM)] * n_pieces,
        out_specs=pl.BlockSpec(memory_space=VMEM),
        scratch_shapes=[
            pltpu.VMEM((2, KVH * 2 * SPAN + WIN, HD), jnp.bfloat16),
            pltpu.VMEM((RD * 16, HD), jnp.bfloat16),
            pltpu.VMEM((RD * 16, HD), jnp.bfloat16),
        ],
        compiler_params=pltpu.CompilerParams(vmem_limit_bytes=LIMIT),
        cost_estimate=pl.CostEstimate(
            flops=24 * 40 * 400 * 128 * 6, bytes_accessed=4 << 20, transcendentals=24 * 40 * 400
        ),
        name="attend",
    )(info, queries, fresh, *pieces)


def unpack_rows(pos, received):
    def kernel(pos_ref, in_ref, out_ref, scr):
        for j in range(RD):
            block = in_ref[pos_ref[j]].astype(jnp.float32)
            for s in range(STEPS):
                rows = pl.ds(s * CH * RD + j, CH, stride=RD)
                for h in range(PER):
                    row = h * TOK + s * CH
                    scr[h, rows, :] = block[row : row + CH]
        for s in range(STEPS):
            for c in range(CH):
                row = (s * CH + c) * RD
                heads = [scr[h, row : row + RD, :] for h in range(PER)]
                out_ref[s, c] = jnp.concatenate(heads, axis=1).astype(jnp.bfloat16)

    return pl.pallas_call(
        kernel,
        out_shape=jax.ShapeDtypeStruct((STEPS, CH, RD, PER * HD), jnp.bfloat16),
        in_specs=[pl.BlockSpec(memory_space=SMEM), pl.BlockSpec(memory_space=VMEM)],
        out_specs=pl.BlockSpec(memory_space=VMEM),
        scratch_shapes=[pltpu.VMEM((PER, TOK * RD, HD), jnp.float32)],
        compiler_params=pltpu.CompilerParams(vmem_limit_bytes=LIMIT),
        cost_estimate=pl.CostEstimate(flops=0, bytes_accessed=1 << 20, transcendentals=0),
        name="unpack_rows",
    )(pos, received)


def body(queries, kv_cache, new_kv, lengths, accepted, dest):
    me_dp = lax.axis_index("dp")
    me_ten = lax.axis_index("tensor")
    z, core = me_ten // 2, me_ten % 2
    n_dp = lax.axis_size("dp")

    def along_z(x, k):
        perm = [(t, (t // 2 + (k if t % 2 == 0 else -k)) % KVH * 2 + t % 2) for t in range(16)]
        return lax.ppermute(x, "tensor", perm)

    def sibling(x):
        return lax.ppermute(x, "tensor", [(t, t ^ 1) for t in range(16)])

    keep, give = split_cache(jnp.stack([z, core]).astype(jnp.int32), kv_cache)
    got = sibling(give)
    moved = [along_z(x, k + 1) for k, x in enumerate(join_cores(keep, got))]
    crossed_a = sibling(jnp.concatenate(moved[:2], axis=0))

    group_of = dest // RD
    order = jnp.arange(RD)
    here = (group_of == me_dp).reshape(n_dp, RD)
    before = jnp.sum(here[:, None, :] & (order[None, :] < order[:, None]), axis=2)
    place = (jnp.arange(n_dp)[:, None] * 2 + before).reshape(-1)
    hit = dest[None, :] == (me_dp * RD + order)[:, None]
    recv_pos = jnp.sum(jnp.where(hit, place[None, :], 0), axis=1)
    taken = jnp.sum(jnp.where(hit[None], accepted[:, None, :], 0), axis=2)
    length = lengths[0]
    start = jnp.sum(jnp.where(order[None, :] < order[:, None], length[None, :], 0), axis=1)
    ident = jnp.where(order == 0, z, jnp.where(order == 1, core, 0))
    info = jnp.stack([recv_pos, start, length, taken[0], taken[1], ident]).astype(jnp.int32)

    first = (me_dp * RD).reshape(1).astype(jnp.int32)
    first, _ = lax.optimization_barrier((first, give))
    by_token = jnp.transpose(queries, (0, 2, 1, 3)), jnp.transpose(new_kv, (0, 1, 3, 2, 4))
    packed, send_pos = pack_rows(dest, first, *by_token)
    received = lax.all_to_all(packed, "dp", split_axis=0, concat_axis=0, tiled=True)
    rows, fresh = pick_rows(info, received)
    crossed_b = sibling(jnp.concatenate(moved[2:] + [fresh], axis=0))
    outs = attend(info, rows, fresh, [give, got] + moved + [crossed_a, crossed_b])
    back = lax.all_to_all(
        outs.reshape(n_dp, 2 * QR, HD), "dp", split_axis=0, concat_axis=0, tiled=True
    )
    out = unpack_rows(send_pos, back.reshape(2 * n_dp, QR, HD))
    return jnp.transpose(out, (0, 2, 1, 3))


def solution(mesh):
    return jax.shard_map(
        body,
        mesh=mesh,
        in_specs=(
            P(None, "dp", None, "tensor"),
            P(None, ("dp", "tensor"), None),
            P(None, None, "dp", None, "tensor"),
            P("dp", None),
            P(),
            P(),
        ),
        out_specs=P(None, "dp", None, "tensor"),
        check_vma=False,
    )
```

time: 101 us -> 92.4 us (0.915)
  the two profiles are of different devices: /device:TPU:64 before, /device:TPU:8 now
where the time goes in v3:
time: 92.4 us; the launch traced here: 91.9 us
  starting transfers between devices  36.6 us (40%)
  blocking collectives  29.6 us (32%)
  waiting for transfers between devices  12.5 us (14%)
  Pallas kernels  9.08 us (10%)
  local copies, waits for them, and re-layouts  2.26 us (2%)
  other arithmetic  1.67 us (2%)
    all_to_all x1, blocking collectives, body(): lax.all_to_all(outs.reshape(n_dp, 2 * QR, HD), 'dp', split_axis=0, concat...  29.6 us
    ppermute x4, starting transfers between devices, along_z(): return lax.ppermute(x, 'tensor', perm)  20.6 us
    ppermute x4, waiting for transfers between devices, along_z(): return lax.ppermute(x, 'tensor', perm)  10.7 us
    all_to_all x1, starting transfers between devices, body(): lax.all_to_all(packed, 'dp', split_axis=0, concat_axis=0, tiled=True)  10.2 us
    ppermute x3, starting transfers between devices, sibling(): return lax.ppermute(x, 'tensor', [(t, t ^ 1) for t in range(16)])  5.75 us
    pallas_call x1, Pallas kernels, attend(): pl.pallas_call(kernel, out_shape=jax.ShapeDtypeStruct((64, QR, HD), jnp.b...  3.2 us
    pallas_call x1, Pallas kernels, pack_rows(): pl.pallas_call(kernel, out_shape=(jax.ShapeDtypeStruct((32, 2 * (QR + TOK...  1.92 us
    unnamed x14, local copies, waits for them, and re-layouts  1.91 us
  transfers between devices with their start and end apart: 8, of which 4 were waited for; matrix products, arithmetic and copies ran while one was open for 2% of the time, Pallas kernels for 4%

profile of v3, /device:TPU:8, one launch (start us, length us, event | category | flops | bytes accessed | tf_op | source)
XLA Modules:
  0.0 91.9 jit_solution(3047593172406261533)
XLA Ops:
  0.0 0.1 pad_add_fusion.id_ref
  0.1 0.0 copy-start
  0.1 1.2 %copy-done = bf16[2,256,1024]{2,1,0:T(8,128)(2,1)S(1)} copy-done((bf16[2,256,1024]{2,1,0:T(8,128)(2,1)S(1)}, bf16[2,256,1024]{2,1,0:T(8,128)(2,1)}, u32[]{:S(2)}) %copy-start) | copy-done | bytes 1048600
  1.3 0.0 copy-start.1
  1.3 0.0 copy-start.2
  1.3 1.0 %split_cache.1 = (bf16[1792,128]{1,0:T(8,128)(2,1)S(1)}, bf16[2304,128]{1,0:T(8,128)(2,1)S(1)}) custom-call(s32[2]{0:T(128)S(1)} %pad_add_fusion.id_ref, bf16[2,256,1024]{2,1,0:T(8,128)(2,1)S(1)} %copy-done), custom_call_target="tpu_custom_call" | custom-call | bytes 2097152 | tf_op jit(solution)/shard_map/split_cache/pallas_call | solution.py:50
  2.3 1.9 %collective-permute-start = (bf16[2304,128]{1,0:T(8,128)(2,1)S(1)}, bf16[2304,128]{1,0:T(8,128)(2,1)S(1)}, u32[]{:S(2)}, u32[]{:S(2)}) collective-permute-start(bf16[2304,128]{1,0:T(8,128)(2,1)S(1)} %get-tuple-element.16.refs_0_), channel_id=1, source_target_pairs={{0,1},{1,0},{2,3},{3,2},{4,5},{5,4},{6,7},{7,6},{8,9},{9,8},{10,11... | collective-permute-start | bytes 1769480 | tf_op jit(solution)/shard_map/ppermute | solution.py:314
  4.3 0.0 copy-start.3
  4.3 0.0 copy-done.1
  4.3 0.0 copy-done.2
  4.3 0.7 copy-done.3
  5.0 1.9 %pack_rows.1 = (bf16[32,100,128]{2,1,0:T(8,128)(2,1)}, s32[24]{0:T(128)S(1)}) custom-call(s32[768]{0:T(1024)S(1)} %copy-done.3, s32[1]{0:T(128)} %bitcast.first_ref, bf16[2,5,24,512]{3,2,1,0:T(8,128)(2,1)S(1)} %bitcast.13, bf16[2,2,5,24,64]{4,3,2,1,0:T(8,128)(2,1)S(1)} %bitcast.14), custom_call_target="tpu_custom_call" | custom-call | bytes 2097152 | tf_op jit(solution)/shard_map/pack_rows/pallas_call | solution.py:113
  6.9 10.2 %all-to-all-start = ((bf16[32,100,128]{2,1,0:T(8,128)(2,1)}), bf16[32,100,128]{2,1,0:T(8,128)(2,1)S(1)}, u32[]{:S(2)}, u32[]{:S(2)}) async-start(bf16[32,100,128]{2,1,0:T(8,128)(2,1)} %get-tuple-element.19), calls=%async_computation | async-start | bytes 1703936 | tf_op jit(solution)/shard_map/all_to_all | solution.py:338
  17.1 0.1 and.34
  17.2 0.1 copy.7
  17.3 0.2 convert_reduce_fusion
  17.5 0.1 copy.8
  17.6 0.1 add.36
  17.7 0.2 select_reduce_fusion.1
  17.8 0.1 broadcast_compare_fusion
  17.9 0.0 collective-permute-done.got_ref.refs_1_
  17.9 0.0 copy-start.6
  18.0 0.8 join_cores.1
  18.7 0.0 copy-start.4
  18.7 0.0 copy-start.5
  18.7 4.4 %collective-permute-start.1 = (bf16[1024,128]{1,0:T(8,128)(2,1)S(1)}, bf16[1024,128]{1,0:T(8,128)(2,1)S(1)}, u32[]{:S(2)}, u32[]{:S(2)}) collective-permute-start(bf16[1024,128]{1,0:T(8,128)(2,1)S(1)} %get-tuple-element.23), channel_id=1, source_target_pairs={{0,2},{1,15},{2,4},{3,1},{4,6},{5,3},{6,8},{7,5},{8,10},{9,7},{10,... | collective-permute-start | bytes 786440 | tf_op jit(solution)/shard_map/ppermute | solution.py:311
  23.1 6.1 %collective-permute-start.2 = (bf16[1024,128]{1,0:T(8,128)(2,1)S(1)}, bf16[1024,128]{1,0:T(8,128)(2,1)S(1)}, u32[]{:S(2)}, u32[]{:S(2)}) collective-permute-start(bf16[1024,128]{1,0:T(8,128)(2,1)S(1)} %get-tuple-element.24), channel_id=1, source_target_pairs={{0,4},{1,13},{2,6},{3,15},{4,8},{5,1},{6,10},{7,3},{8,12},{9,5},{1... | collective-permute-start | bytes 786440 | tf_op jit(solution)/shard_map/ppermute | solution.py:311
  29.2 0.0 copy-done.6
  29.2 0.1 select_reduce_fusion.2
  29.4 0.0 copy-done.5
  29.4 0.1 select_reduce_fusion
  29.5 7.3 %collective-permute-start.3 = (bf16[1024,128]{1,0:T(8,128)(2,1)}, bf16[1024,128]{1,0:T(8,128)(2,1)S(1)}, u32[]{:S(2)}, u32[]{:S(2)}) collective-permute-start(bf16[1024,128]{1,0:T(8,128)(2,1)} %get-tuple-element.25), channel_id=1, source_target_pairs={{0,6},{1,11},{2,8},{3,13},{4,10},{5,15},{6,12},{7,1},{8,14},{9,3},... | collective-permute-start | bytes 786440 | tf_op jit(solution)/shard_map/ppermute | solution.py:311
  36.8 0.0 copy-done.4
  36.8 2.8 %collective-permute-start.4 = (bf16[512,128]{1,0:T(8,128)(2,1)}, bf16[512,128]{1,0:T(8,128)(2,1)S(1)}, u32[]{:S(2)}, u32[]{:S(2)}) collective-permute-start(bf16[512,128]{1,0:T(8,128)(2,1)} %copy-done.4), channel_id=1, source_target_pairs={{0,8},{1,9},{2,10},{3,11},{4,12},{5,13},{6,14},{7,15},{8,0},{9,1},... | collective-permute-start | bytes 393224 | tf_op jit(solution)/shard_map/ppermute | solution.py:311
  39.7 0.0 collective-permute-done.1.refs_2_
  39.7 3.3 %collective-permute-done.2.refs_3_ = bf16[1024,128]{1,0:T(8,128)(2,1)S(1)} collective-permute-done((bf16[1024,128]{1,0:T(8,128)(2,1)S(1)}, bf16[1024,128]{1,0:T(8,128)(2,1)S(1)}, u32[]{:S(2)}, u32[]{:S(2)}) %collective-permute-start.2) | collective-permute-done | bytes 262176 | tf_op jit(solution)/shard_map/ppermute | solution.py:311
  43.0 0.9 pad_maximum_fusion
  43.8 1.9 %collective-permute-start.5 = (bf16[2048,128]{1,0:T(8,128)(2,1)}, bf16[2048,128]{1,0:T(8,128)(2,1)S(1)}, u32[]{:S(2)}, u32[]{:S(2)}) collective-permute-start(bf16[2048,128]{1,0:T(8,128)(2,1)} %pad_maximum_fusion), channel_id=1, source_target_pairs={{0,1},{1,0},{2,3},{3,2},{4,5},{5,4},{6,7},{7,6},{8,9},{9,8},{10,11... | collective-permute-start | bytes 1572872 | tf_op jit(solution)/shard_map/ppermute | solution.py:314
  45.7 0.0 all-to-all-done.recv_ref
  45.7 0.8 pick_rows.1
  46.5 7.2 %collective-permute-done.4.refs_5_ = bf16[512,128]{1,0:T(8,128)(2,1)S(1)} collective-permute-done((bf16[512,128]{1,0:T(8,128)(2,1)}, bf16[512,128]{1,0:T(8,128)(2,1)S(1)}, u32[]{:S(2)}, u32[]{:S(2)}) %collective-permute-start.4) | collective-permute-done | bytes 131104 | tf_op jit(solution)/shard_map/ppermute | solution.py:311
  53.7 0.2 collective-permute-done.3.refs_4_
  53.9 1.9 %collective-permute-start.6 = (bf16[1920,128]{1,0:T(8,128)(2,1)S(1)}, bf16[1920,128]{1,0:T(8,128)(2,1)S(1)}, u32[]{:S(2)}, u32[]{:S(2)}) collective-permute-start(bf16[1920,128]{1,0:T(8,128)(2,1)S(1)} %pad_maximum_fusion.1), channel_id=1, source_target_pairs={{0,1},{1,0},{2,3},{3,2},{4,5},{5,4},{6,7},{7,6},{8,9},{9,8},{10,11... | collective-permute-start | bytes 1474568 | tf_op jit(solution)/shard_map/ppermute | solution.py:314
  55.9 0.0 collective-permute-done.5.refs_6_
  55.9 1.8 %collective-permute-done.6.refs_7_ = bf16[1920,128]{1,0:T(8,128)(2,1)S(1)} collective-permute-done((bf16[1920,128]{1,0:T(8,128)(2,1)S(1)}, bf16[1920,128]{1,0:T(8,128)(2,1)S(1)}, u32[]{:S(2)}, u32[]{:S(2)}) %collective-permute-start.6) | collective-permute-done | bytes 491552 | tf_op jit(solution)/shard_map/ppermute | solution.py:314
  57.7 3.2 %attend.1 = bf16[64,40,128]{2,1,0:T(8,128)(2,1)S(1)} custom-call(s32[6,24]{1,0:T(8,128)S(1)} %stack.24.info_ref, bf16[24,40,128]{2,1,0:T(8,128)(2,1)S(1)} %get-tuple-element.20.qs, bf16[384,128]{1,0:T(8,128)(2,1)S(1)} %get-tuple-element.21.fresh_ref, bf16[2304,128]{1,0:T(8,128)(2,1)S(1)} %get-tuple-element.16.refs_0_, ...), custom_call_target="tpu_custom_call" | custom-call | flops 294912000 | bytes 4194304 | tf_op jit(solution)/shard_map/attend/pallas_call | solution.py:253
  60.9 29.6 %all_to_all.10 = bf16[32,80,128]{2,1,0:T(8,128)(2,1)S(1)} all-to-all(bf16[32,80,128]{2,1,0:T(8,128)(2,1)S(1)} %bitcast.11), channel_id=1, replica_groups=mesh['dp'=32,'tensor'=16] {'dp'}, dimensions={0} | all-to-all | bytes 1310720 | tf_op jit(solution)/shard_map/all_to_all | solution.py:342
  90.5 1.4 %unpack_rows.1 = bf16[2,5,24,512]{3,2,1,0:T(8,128)(2,1)} custom-call(s32[24]{0:T(128)S(1)} %get-tuple-element.18.pos_ref, bf16[64,40,128]{2,1,0:T(8,128)(2,1)S(1)} %bitcast.12), custom_call_target="tpu_custom_call" | custom-call | bytes 1048576 | tf_op jit(solution)/shard_map/unpack_rows/pallas_call | solution.py:291
  (8 shorter events, 0.1 us)
Async XLA Ops:
  0.1 1.2 %copy-start = (bf16[2,256,1024]{2,1,0:T(8,128)(2,1)S(1)}, bf16[2,256,1024]{2,1,0:T(8,128)(2,1)}, u32[]{:S(2)}) copy-start(bf16[2,256,1024]{2,1,0:T(8,128)(2,1)} %kv_ref.1) | copy-start | bytes 3145732
  1.3 3.0 %copy-start.1 = (bf16[2,24,5,512]{3,1,2,0:T(8,128)(2,1)S(1)}, bf16[2,24,5,512]{3,1,2,0:T(8,128)(2,1)}, u32[]{:S(2)}) copy-start(bf16[2,24,5,512]{3,1,2,0:T(8,128)(2,1)} %param.6) | copy-start | bytes 737284
  1.3 3.0 %copy-start.2 = (bf16[2,2,24,5,64]{4,2,3,1,0:T(8,128)(2,1)S(1)}, bf16[2,2,24,5,64]{4,2,3,1,0:T(8,128)(2,1)}, u32[]{:S(2)}) copy-start(bf16[2,2,24,5,64]{4,2,3,1,0:T(8,128)(2,1)} %param.8) | copy-start | bytes 184324
  2.3 15.6 %collective-permute-start = (bf16[2304,128]{1,0:T(8,128)(2,1)S(1)}, bf16[2304,128]{1,0:T(8,128)(2,1)S(1)}, u32[]{:S(2)}, u32[]{:S(2)}) collective-permute-start(bf16[2304,128]{1,0:T(8,128)(2,1)S(1)} %get-tuple-element.16.refs_0_), channel_id=1, source_target_pairs={{0,1},{1,0},{2,3},{3,2},{4,5},{5,4},{6,7},{7,6},{8,9},{9,8},{10,11... | collective-permute-start | bytes 1769480 | tf_op jit(solution)/shard_map/ppermute | solution.py:314
  4.3 0.7 copy-start.3
  6.9 38.8 %all-to-all-start = ((bf16[32,100,128]{2,1,0:T(8,128)(2,1)}), bf16[32,100,128]{2,1,0:T(8,128)(2,1)S(1)}, u32[]{:S(2)}, u32[]{:S(2)}) async-start(bf16[32,100,128]{2,1,0:T(8,128)(2,1)} %get-tuple-element.19), calls=%async_computation | async-start | bytes 1703936 | tf_op jit(solution)/shard_map/all_to_all | solution.py:338
  17.9 11.3 %copy-start.6 = (s32[1,24]{1,0:T(1,128)S(1)}, s32[1,24]{1,0:T(1,128)}, u32[]{:S(2)}) copy-start(s32[1,24]{1,0:T(1,128)} %param.9) | copy-start | bytes 292
  18.7 18.1 %copy-start.4 = (bf16[512,128]{1,0:T(8,128)(2,1)}, bf16[512,128]{1,0:T(8,128)(2,1)S(1)}, u32[]{:S(2)}) copy-start(bf16[512,128]{1,0:T(8,128)(2,1)S(1)} %get-tuple-element.26) | copy-start | bytes 393220
  18.7 10.6 %copy-start.5 = (s32[2,768]{1,0:T(2,128)S(1)}, s32[2,768]{1,0:T(2,128)}, u32[]{:S(2)}) copy-start(s32[2,768]{1,0:T(2,128)} %param.10) | copy-start | bytes 18436
  18.7 21.0 %collective-permute-start.1 = (bf16[1024,128]{1,0:T(8,128)(2,1)S(1)}, bf16[1024,128]{1,0:T(8,128)(2,1)S(1)}, u32[]{:S(2)}, u32[]{:S(2)}) collective-permute-start(bf16[1024,128]{1,0:T(8,128)(2,1)S(1)} %get-tuple-element.23), channel_id=1, source_target_pairs={{0,2},{1,15},{2,4},{3,1},{4,6},{5,3},{6,8},{7,5},{8,10},{9,7},{10,... | collective-permute-start | bytes 786440 | tf_op jit(solution)/shard_map/ppermute | solution.py:311
  23.1 19.8 %collective-permute-start.2 = (bf16[1024,128]{1,0:T(8,128)(2,1)S(1)}, bf16[1024,128]{1,0:T(8,128)(2,1)S(1)}, u32[]{:S(2)}, u32[]{:S(2)}) collective-permute-start(bf16[1024,128]{1,0:T(8,128)(2,1)S(1)} %get-tuple-element.24), channel_id=1, source_target_pairs={{0,4},{1,13},{2,6},{3,15},{4,8},{5,1},{6,10},{7,3},{8,12},{9,5},{1... | collective-permute-start | bytes 786440 | tf_op jit(solution)/shard_map/ppermute | solution.py:311
  29.5 24.4 %collective-permute-start.3 = (bf16[1024,128]{1,0:T(8,128)(2,1)}, bf16[1024,128]{1,0:T(8,128)(2,1)S(1)}, u32[]{:S(2)}, u32[]{:S(2)}) collective-permute-start(bf16[1024,128]{1,0:T(8,128)(2,1)} %get-tuple-element.25), channel_id=1, source_target_pairs={{0,6},{1,11},{2,8},{3,13},{4,10},{5,15},{6,12},{7,1},{8,14},{9,3},... | collective-permute-start | bytes 786440 | tf_op jit(solution)/shard_map/ppermute | solution.py:311
  36.8 16.9 %collective-permute-start.4 = (bf16[512,128]{1,0:T(8,128)(2,1)}, bf16[512,128]{1,0:T(8,128)(2,1)S(1)}, u32[]{:S(2)}, u32[]{:S(2)}) collective-permute-start(bf16[512,128]{1,0:T(8,128)(2,1)} %copy-done.4), channel_id=1, source_target_pairs={{0,8},{1,9},{2,10},{3,11},{4,12},{5,13},{6,14},{7,15},{8,0},{9,1},... | collective-permute-start | bytes 393224 | tf_op jit(solution)/shard_map/ppermute | solution.py:311
  43.8 12.1 %collective-permute-start.5 = (bf16[2048,128]{1,0:T(8,128)(2,1)}, bf16[2048,128]{1,0:T(8,128)(2,1)S(1)}, u32[]{:S(2)}, u32[]{:S(2)}) collective-permute-start(bf16[2048,128]{1,0:T(8,128)(2,1)} %pad_maximum_fusion), channel_id=1, source_target_pairs={{0,1},{1,0},{2,3},{3,2},{4,5},{5,4},{6,7},{7,6},{8,9},{9,8},{10,11... | collective-permute-start | bytes 1572872 | tf_op jit(solution)/shard_map/ppermute | solution.py:314
  53.9 3.8 %collective-permute-start.6 = (bf16[1920,128]{1,0:T(8,128)(2,1)S(1)}, bf16[1920,128]{1,0:T(8,128)(2,1)S(1)}, u32[]{:S(2)}, u32[]{:S(2)}) collective-permute-start(bf16[1920,128]{1,0:T(8,128)(2,1)S(1)} %pad_maximum_fusion.1), channel_id=1, source_target_pairs={{0,1},{1,0},{2,3},{3,2},{4,5},{5,4},{6,7},{7,6},{8,9},{9,8},{10,11... | collective-permute-start | bytes 1474568 | tf_op jit(solution)/shard_map/ppermute | solution.py:314

commit v4 on v3

--- a/solution.py
+++ b/solution.py
@@ -16,6 +16,7 @@
 TOK = STEPS * CH
 PER = 4
 QR = PER * TOK
+PITCH = 56
 SCALE = HD**-0.5
 VMEM = pltpu.MemorySpace.VMEM
 SMEM = pltpu.MemorySpace.SMEM
@@ -23,16 +24,13 @@
 
 
 def split_cache(ident, kv):
-    def kernel(id_ref, kv_ref, keep_ref, give_ref, sems):
+    def kernel(id_ref, kv_ref, keep_ref, give_ref):
         z, core = id_ref[0], id_ref[1]
         step = 1 - 2 * core
-        copies = []
 
         def put(ref, unit, side, dist):
             col = pl.multiple_of(lax.rem(z + dist + KVH, KVH) * HD, HD)
-            src = kv_ref.at[side, :, pl.ds(col, HD)]
-            dst = ref.at[pl.ds(unit * SPAN, SPAN)]
-            copies.append(pltpu.make_async_copy(src, dst, sems.at[len(copies)]))
+            ref[unit * SPAN : (unit + 1) * SPAN, :] = kv_ref[side, :, pl.ds(col, HD)]
 
         for dist in range(1, 4):
             for side in range(2):
@@ -42,10 +40,6 @@
         put(keep_ref, 6, core, 4)
         put(give_ref, 7, 0, 0)
         put(give_ref, 8, 1, 0)
-        for copy in copies:
-            copy.start()
-        for copy in copies:
-            copy.wait()
 
     return pl.pallas_call(
         kernel,
@@ -53,9 +47,8 @@
             jax.ShapeDtypeStruct((7 * SPAN, HD), kv.dtype),
             jax.ShapeDtypeStruct((9 * SPAN, HD), kv.dtype),
         ),
-        in_specs=[pl.BlockSpec(memory_space=SMEM), pl.BlockSpec(memory_space=pl.ANY)],
+        in_specs=[pl.BlockSpec(memory_space=SMEM), pl.BlockSpec(memory_space=VMEM)],
         out_specs=[pl.BlockSpec(memory_space=VMEM)] * 2,
-        scratch_shapes=[pltpu.SemaphoreType.DMA((16,))],
         compiler_params=pltpu.CompilerParams(vmem_limit_bytes=LIMIT),
         cost_estimate=pl.CostEstimate(flops=0, bytes_accessed=2 << 20, transcendentals=0),
         name="split_cache",
@@ -83,7 +76,7 @@
 
 
 def pack_rows(dest, first, queries, new_kv):
-    def kernel(dest_ref, first_ref, q_ref, n_ref, out_ref, pos_ref, seen, qf, nf, qs, ns):
+    def kernel(dest_ref, first_ref, q_ref, n_ref, out_ref, pos_ref, seen, flat, qs, ns):
         for g in range(32):
             seen[g] = 0
         for j in range(RD):
@@ -92,20 +85,17 @@
             seen[g] = 1
         for s in range(STEPS):
             for c in range(CH):
-                row = (s * CH + c) * RD
+                row = s * CH + c
                 q = q_ref[s, c].astype(jnp.float32)
                 for h in range(PER):
-                    qf[h, row : row + RD, :] = q[:, h * HD : (h + 1) * HD]
+                    rows = pl.ds(h * TOK + row, RD, stride=PITCH)
+                    flat[rows, :] = q[:, h * HD : (h + 1) * HD]
                 n = [n_ref[side, s, c].astype(jnp.float32) for side in range(2)]
-                nf[row : row + RD, :] = jnp.concatenate(n, axis=1)
+                flat[pl.ds(QR + row, RD, stride=PITCH), :] = jnp.concatenate(n, axis=1)
         for j in range(RD):
             at = pos_ref[j]
-            for s in range(STEPS):
-                rows = pl.ds(s * CH * RD + j, CH, stride=RD)
-                for h in range(PER):
-                    row = h * TOK + s * CH
-                    qs[at, row : row + CH, :] = qf[h, rows, :]
-                ns[at, s * CH : (s + 1) * CH, :] = nf[rows, :]
+            qs[at] = flat[j * PITCH : j * PITCH + QR, :]
+            ns[at] = flat[j * PITCH + QR : j * PITCH + QR + TOK, :]
         for g in range(32):
             block = [qs[2 * g], qs[2 * g + 1], ns[2 * g], ns[2 * g + 1]]
             out_ref[g] = jnp.concatenate(block, axis=0).astype(jnp.bfloat16)
@@ -125,8 +115,7 @@
         out_specs=(pl.BlockSpec(memory_space=VMEM), pl.BlockSpec(memory_space=SMEM)),
         scratch_shapes=[
             pltpu.SMEM((32,), jnp.int32),
-            pltpu.VMEM((PER, TOK * RD, HD), jnp.float32),
-            pltpu.VMEM((TOK * RD, HD), jnp.float32),
+            pltpu.VMEM((RD * PITCH, HD), jnp.float32),
             pltpu.VMEM((64, QR, HD), jnp.float32),
             pltpu.VMEM((64, TOK, HD), jnp.float32),
         ],
@@ -209,46 +198,39 @@
         kn[...] = jnp.where(low_half, low, pltpu.roll(high, HD // 2, 1)).astype(jnp.bfloat16)
         vn[...] = jnp.where(low_half, pltpu.roll(low, HD // 2, 1), high).astype(jnp.bfloat16)
 
-        group = 12
-
-        def some(it, carry):
-            js = [it * group + i for i in range(group)]
-            scores, values = [], []
-            for j in js:
-                start, length = info_ref[1, j], info_ref[2, j]
-                base = pl.multiple_of((start // 16) * 16, 16)
-                off = start - base
-                keys = jnp.concatenate([kvbuf[0, pl.ds(base, WIN), :], kn[pl.ds(16 * j, 16), :]], axis=0)
-                sc = lax.dot_general(
-                    qs[j], keys, (((1,), (1,)), ((), ())), preferred_element_type=jnp.float32
-                )
-                cached = jnp.where(
-                    (col >= off) & (col < off + length), sc[:, :WIN] * SCALE, -1e30
-                )
-                fresh = jnp.where(need <= info_ref[3, j], sc[:, WIN:] * SCALE, -1e30)
-                scores.append((cached, fresh))
-            weights = []
-            for cached, fresh in scores:
-                top = jnp.maximum(
-                    jnp.max(cached, axis=1, keepdims=True), jnp.max(fresh, axis=1, keepdims=True)
-                )
-                wc, wf = jnp.exp(cached - top), jnp.exp(fresh - top)
-                total = jnp.sum(wc, axis=1, keepdims=True) + jnp.sum(wf, axis=1, keepdims=True)
-                weights.append((jnp.concatenate([wc, wf], axis=1), total))
-            for j, (w, total) in zip(js, weights):
-                base = pl.multiple_of((info_ref[1, j] // 16) * 16, 16)
-                vals = jnp.concatenate([kvbuf[1, pl.ds(base, WIN), :], vn[pl.ds(16 * j, 16), :]], axis=0)
-                high = w.astype(jnp.bfloat16)
-                low = (w - high.astype(jnp.float32)).astype(jnp.bfloat16)
-                dims = (((1,), (0,)), ((), ()))
-                acc = lax.dot_general(high, vals, dims, preferred_element_type=jnp.float32)
-                acc += lax.dot_general(low, vals, dims, preferred_element_type=jnp.float32)
-                limit = jnp.where(tstep == 0, info_ref[3, j], info_ref[4, j])
-                out = jnp.where(tpos <= limit, acc / total, 0.0)
-                out_ref[info_ref[0, j]] = out.astype(jnp.bfloat16)
-            return carry
-
-        lax.fori_loop(0, RD // group, some, 0)
+        scores, weights = [], []
+        for j in range(RD):
+            start, length = info_ref[1, j], info_ref[2, j]
+            base = pl.multiple_of((start // 16) * 16, 16)
+            off = start - base
+            keys = jnp.concatenate([kvbuf[0, pl.ds(base, WIN), :], kn[pl.ds(16 * j, 16), :]], axis=0)
+            sc = lax.dot_general(
+                qs[j], keys, (((1,), (1,)), ((), ())), preferred_element_type=jnp.float32
+            )
+            cached = jnp.where(
+                (col >= off) & (col < off + length), sc[:, :WIN] * SCALE, -1e30
+            )
+            fresh = jnp.where(need <= info_ref[3, j], sc[:, WIN:] * SCALE, -1e30)
+            scores.append((cached, fresh))
+        for cached, fresh in scores:
+            top = jnp.maximum(
+                jnp.max(cached, axis=1, keepdims=True), jnp.max(fresh, axis=1, keepdims=True)
+            )
+            wc, wf = jnp.exp(cached - top), jnp.exp(fresh - top)
+            total = jnp.sum(wc, axis=1, keepdims=True) + jnp.sum(wf, axis=1, keepdims=True)
+            weights.append((jnp.concatenate([wc, wf], axis=1), total))
+        for j, (w, total) in enumerate(weights):
+            base = pl.multiple_of((info_ref[1, j] // 16) * 16, 16)
+            vals = jnp.concatenate([kvbuf[1, pl.ds(base, WIN), :], vn[pl.ds(16 * j, 16), :]], axis=0)
+            high = w.astype(jnp.bfloat16)
+            low = (w - high.astype(jnp.float32)).astype(jnp.bfloat16)
+            dims = (((1,), (0,)), ((), ()))
+            both = jnp.concatenate([high, low], axis=0)
+            both = lax.dot_general(both, vals, dims, preferred_element_type=jnp.float32)
+            acc = both[:QR] + both[QR:]
+            limit = jnp.where(tstep == 0, info_ref[3, j], info_ref[4, j])
+            out = jnp.where(tpos <= limit, acc / total, 0.0)
+            out_ref[info_ref[0, j]] = out.astype(jnp.bfloat16)
 
     return pl.pallas_call(
         kernel,
@@ -276,16 +258,11 @@
 def unpack_rows(pos, received):
     def kernel(pos_ref, in_ref, out_ref, scr):
         for j in range(RD):
-            block = in_ref[pos_ref[j]].astype(jnp.float32)
-            for s in range(STEPS):
-                rows = pl.ds(s * CH * RD + j, CH, stride=RD)
-                for h in range(PER):
-                    row = h * TOK + s * CH
-                    scr[h, rows, :] = block[row : row + CH]
+            scr[j * QR : (j + 1) * QR, :] = in_ref[pos_ref[j]].astype(jnp.float32)
         for s in range(STEPS):
             for c in range(CH):
-                row = (s * CH + c) * RD
-                heads = [scr[h, row : row + RD, :] for h in range(PER)]
+                at = s * CH + c
+                heads = [scr[pl.ds(h * TOK + at, RD, stride=QR), :] for h in range(PER)]
                 out_ref[s, c] = jnp.concatenate(heads, axis=1).astype(jnp.bfloat16)
 
     return pl.pallas_call(
@@ -293,7 +270,7 @@
         out_shape=jax.ShapeDtypeStruct((STEPS, CH, RD, PER * HD), jnp.bfloat16),
         in_specs=[pl.BlockSpec(memory_space=SMEM), pl.BlockSpec(memory_space=VMEM)],
         out_specs=pl.BlockSpec(memory_space=VMEM),
-        scratch_shapes=[pltpu.VMEM((PER, TOK * RD, HD), jnp.float32)],
+        scratch_shapes=[pltpu.VMEM((RD * QR, HD), jnp.float32)],
         compiler_params=pltpu.CompilerParams(vmem_limit_bytes=LIMIT),
         cost_estimate=pl.CostEstimate(flops=0, bytes_accessed=1 << 20, transcendentals=0),
         name="unpack_rows",

time: 92.4 us -> 91.6 us (level)
  no operation moved by 1% of the time
where the time goes in v4:
time: 91.6 us; the launch traced here: 91.1 us
  starting transfers between devices  36.6 us (40%)
  blocking collectives  29.6 us (32%)
  waiting for transfers between devices  12.5 us (14%)
  Pallas kernels  8.22 us (9%)
  local copies, waits for them, and re-layouts  2.26 us (2%)
  other arithmetic  1.67 us (2%)
    all_to_all x1, blocking collectives, body(): lax.all_to_all(outs.reshape(n_dp, 2 * QR, HD), 'dp', split_axis=0, concat...  29.6 us
    ppermute x4, starting transfers between devices, along_z(): return lax.ppermute(x, 'tensor', perm)  20.6 us
    ppermute x4, waiting for transfers between devices, along_z(): return lax.ppermute(x, 'tensor', perm)  10.7 us
    all_to_all x1, starting transfers between devices, body(): lax.all_to_all(packed, 'dp', split_axis=0, concat_axis=0, tiled=True)  10.2 us
    ppermute x3, starting transfers between devices, sibling(): return lax.ppermute(x, 'tensor', [(t, t ^ 1) for t in range(16)])  5.75 us
    pallas_call x1, Pallas kernels, attend(): pl.pallas_call(kernel, out_shape=jax.ShapeDtypeStruct((64, QR, HD), jnp.b...  2.67 us
    unnamed x14, local copies, waits for them, and re-layouts  1.91 us
    pallas_call x1, Pallas kernels, pack_rows(): pl.pallas_call(kernel, out_shape=(jax.ShapeDtypeStruct((32, 2 * (QR + TOK...  1.86 us
  transfers between devices with their start and end apart: 8, of which 4 were waited for; matrix products, arithmetic and copies ran while one was open for 2% of the time, Pallas kernels for 4%

profile of v4, /device:TPU:8, one launch (start us, length us, event | category | flops | bytes accessed | tf_op | source)
XLA Modules:
  0.0 91.1 jit_solution(17897260976172786217)
XLA Ops:
  0.0 0.1 pad_add_fusion.id_ref
  0.1 0.0 copy-start
  0.1 1.2 %copy-done = bf16[2,256,1024]{2,1,0:T(8,128)(2,1)S(1)} copy-done((bf16[2,256,1024]{2,1,0:T(8,128)(2,1)S(1)}, bf16[2,256,1024]{2,1,0:T(8,128)(2,1)}, u32[]{:S(2)}) %copy-start) | copy-done | bytes 1048600
  1.3 0.0 copy-start.1
  1.3 0.0 copy-start.2
  1.3 0.8 split_cache.1
  2.1 1.9 %collective-permute-start = (bf16[2304,128]{1,0:T(8,128)(2,1)S(1)}, bf16[2304,128]{1,0:T(8,128)(2,1)S(1)}, u32[]{:S(2)}, u32[]{:S(2)}) collective-permute-start(bf16[2304,128]{1,0:T(8,128)(2,1)S(1)} %get-tuple-element.16.refs_0_), channel_id=1, source_target_pairs={{0,1},{1,0},{2,3},{3,2},{4,5},{5,4},{6,7},{7,6},{8,9},{9,8},{10,11... | collective-permute-start | bytes 1769480 | tf_op jit(solution)/shard_map/ppermute | solution.py:291
  4.1 0.0 copy-start.3
  4.1 0.0 copy-done.1
  4.1 0.0 copy-done.2
  4.1 0.7 copy-done.3
  4.8 1.9 %pack_rows.1 = (bf16[32,100,128]{2,1,0:T(8,128)(2,1)}, s32[24]{0:T(128)S(1)}) custom-call(s32[768]{0:T(1024)S(1)} %copy-done.3, s32[1]{0:T(128)} %bitcast.first_ref, bf16[2,5,24,512]{3,2,1,0:T(8,128)(2,1)S(1)} %bitcast.13, bf16[2,2,5,24,64]{4,3,2,1,0:T(8,128)(2,1)S(1)} %bitcast.14), custom_call_target="tpu_custom_call" | custom-call | bytes 2097152 | tf_op jit(solution)/shard_map/pack_rows/pallas_call | solution.py:103
  6.6 10.2 %all-to-all-start = ((bf16[32,100,128]{2,1,0:T(8,128)(2,1)}), bf16[32,100,128]{2,1,0:T(8,128)(2,1)S(1)}, u32[]{:S(2)}, u32[]{:S(2)}) async-start(bf16[32,100,128]{2,1,0:T(8,128)(2,1)} %get-tuple-element.19), calls=%async_computation | async-start | bytes 1703936 | tf_op jit(solution)/shard_map/all_to_all | solution.py:315
  16.8 0.1 and.34
  16.9 0.1 copy.7
  17.0 0.2 convert_reduce_fusion
  17.2 0.1 copy.8
  17.3 0.1 add.36
  17.4 0.2 select_reduce_fusion.1
  17.6 0.1 broadcast_compare_fusion
  17.7 0.0 collective-permute-done.got_ref.refs_1_
  17.7 0.0 copy-start.6
  17.7 0.8 join_cores.1
  18.5 0.0 copy-start.4
  18.5 0.0 copy-start.5
  18.5 4.4 %collective-permute-start.1 = (bf16[1024,128]{1,0:T(8,128)(2,1)S(1)}, bf16[1024,128]{1,0:T(8,128)(2,1)S(1)}, u32[]{:S(2)}, u32[]{:S(2)}) collective-permute-start(bf16[1024,128]{1,0:T(8,128)(2,1)S(1)} %get-tuple-element.23), channel_id=1, source_target_pairs={{0,2},{1,15},{2,4},{3,1},{4,6},{5,3},{6,8},{7,5},{8,10},{9,7},{10,... | collective-permute-start | bytes 786440 | tf_op jit(solution)/shard_map/ppermute | solution.py:288
  22.9 6.1 %collective-permute-start.2 = (bf16[1024,128]{1,0:T(8,128)(2,1)S(1)}, bf16[1024,128]{1,0:T(8,128)(2,1)S(1)}, u32[]{:S(2)}, u32[]{:S(2)}) collective-permute-start(bf16[1024,128]{1,0:T(8,128)(2,1)S(1)} %get-tuple-element.24), channel_id=1, source_target_pairs={{0,4},{1,13},{2,6},{3,15},{4,8},{5,1},{6,10},{7,3},{8,12},{9,5},{1... | collective-permute-start | bytes 786440 | tf_op jit(solution)/shard_map/ppermute | solution.py:288
  29.0 0.0 copy-done.6
  29.0 0.1 select_reduce_fusion.2
  29.1 0.0 copy-done.5
  29.1 0.1 select_reduce_fusion
  29.2 7.3 %collective-permute-start.3 = (bf16[1024,128]{1,0:T(8,128)(2,1)}, bf16[1024,128]{1,0:T(8,128)(2,1)S(1)}, u32[]{:S(2)}, u32[]{:S(2)}) collective-permute-start(bf16[1024,128]{1,0:T(8,128)(2,1)} %get-tuple-element.25), channel_id=1, source_target_pairs={{0,6},{1,11},{2,8},{3,13},{4,10},{5,15},{6,12},{7,1},{8,14},{9,3},... | collective-permute-start | bytes 786440 | tf_op jit(solution)/shard_map/ppermute | solution.py:288
  36.6 0.0 copy-done.4
  36.6 2.8 %collective-permute-start.4 = (bf16[512,128]{1,0:T(8,128)(2,1)}, bf16[512,128]{1,0:T(8,128)(2,1)S(1)}, u32[]{:S(2)}, u32[]{:S(2)}) collective-permute-start(bf16[512,128]{1,0:T(8,128)(2,1)} %copy-done.4), channel_id=1, source_target_pairs={{0,8},{1,9},{2,10},{3,11},{4,12},{5,13},{6,14},{7,15},{8,0},{9,1},... | collective-permute-start | bytes 393224 | tf_op jit(solution)/shard_map/ppermute | solution.py:288
  39.4 0.0 collective-permute-done.1.refs_2_
  39.4 3.3 %collective-permute-done.2.refs_3_ = bf16[1024,128]{1,0:T(8,128)(2,1)S(1)} collective-permute-done((bf16[1024,128]{1,0:T(8,128)(2,1)S(1)}, bf16[1024,128]{1,0:T(8,128)(2,1)S(1)}, u32[]{:S(2)}, u32[]{:S(2)}) %collective-permute-start.2) | collective-permute-done | bytes 262176 | tf_op jit(solution)/shard_map/ppermute | solution.py:288
  42.7 0.9 pad_maximum_fusion
  43.5 1.9 %collective-permute-start.5 = (bf16[2048,128]{1,0:T(8,128)(2,1)}, bf16[2048,128]{1,0:T(8,128)(2,1)S(1)}, u32[]{:S(2)}, u32[]{:S(2)}) collective-permute-start(bf16[2048,128]{1,0:T(8,128)(2,1)} %pad_maximum_fusion), channel_id=1, source_target_pairs={{0,1},{1,0},{2,3},{3,2},{4,5},{5,4},{6,7},{7,6},{8,9},{9,8},{10,11... | collective-permute-start | bytes 1572872 | tf_op jit(solution)/shard_map/ppermute | solution.py:291
  45.5 0.0 all-to-all-done.recv_ref
  45.5 0.8 pick_rows.1
  46.2 7.2 %collective-permute-done.4.refs_5_ = bf16[512,128]{1,0:T(8,128)(2,1)S(1)} collective-permute-done((bf16[512,128]{1,0:T(8,128)(2,1)}, bf16[512,128]{1,0:T(8,128)(2,1)S(1)}, u32[]{:S(2)}, u32[]{:S(2)}) %collective-permute-start.4) | collective-permute-done | bytes 131104 | tf_op jit(solution)/shard_map/ppermute | solution.py:288
  53.5 0.2 collective-permute-done.3.refs_4_
  53.7 1.9 %collective-permute-start.6 = (bf16[1920,128]{1,0:T(8,128)(2,1)S(1)}, bf16[1920,128]{1,0:T(8,128)(2,1)S(1)}, u32[]{:S(2)}, u32[]{:S(2)}) collective-permute-start(bf16[1920,128]{1,0:T(8,128)(2,1)S(1)} %pad_maximum_fusion.1), channel_id=1, source_target_pairs={{0,1},{1,0},{2,3},{3,2},{4,5},{5,4},{6,7},{7,6},{8,9},{9,8},{10,11... | collective-permute-start | bytes 1474568 | tf_op jit(solution)/shard_map/ppermute | solution.py:291
  55.6 0.0 collective-permute-done.5.refs_6_
  55.6 1.8 %collective-permute-done.6.refs_7_ = bf16[1920,128]{1,0:T(8,128)(2,1)S(1)} collective-permute-done((bf16[1920,128]{1,0:T(8,128)(2,1)S(1)}, bf16[1920,128]{1,0:T(8,128)(2,1)S(1)}, u32[]{:S(2)}, u32[]{:S(2)}) %collective-permute-start.6) | collective-permute-done | bytes 491552 | tf_op jit(solution)/shard_map/ppermute | solution.py:291
  57.4 2.7 %attend.1 = bf16[64,40,128]{2,1,0:T(8,128)(2,1)S(1)} custom-call(s32[6,24]{1,0:T(8,128)S(1)} %stack.24.info_ref, bf16[24,40,128]{2,1,0:T(8,128)(2,1)S(1)} %get-tuple-element.20.qs, bf16[384,128]{1,0:T(8,128)(2,1)S(1)} %get-tuple-element.21.fresh_ref, bf16[2304,128]{1,0:T(8,128)(2,1)S(1)} %get-tuple-element.16.refs_0_, ...), custom_call_target="tpu_custom_call" | custom-call | flops 294912000 | bytes 4194304 | tf_op jit(solution)/shard_map/attend/pallas_call | solution.py:235
  60.1 29.6 %all_to_all.10 = bf16[32,80,128]{2,1,0:T(8,128)(2,1)S(1)} all-to-all(bf16[32,80,128]{2,1,0:T(8,128)(2,1)S(1)} %bitcast.11), channel_id=1, replica_groups=mesh['dp'=32,'tensor'=16] {'dp'}, dimensions={0} | all-to-all | bytes 1310720 | tf_op jit(solution)/shard_map/all_to_all | solution.py:319
  89.7 1.4 %unpack_rows.1 = bf16[2,5,24,512]{3,2,1,0:T(8,128)(2,1)} custom-call(s32[24]{0:T(128)S(1)} %get-tuple-element.18.pos_ref, bf16[64,40,128]{2,1,0:T(8,128)(2,1)S(1)} %bitcast.12), custom_call_target="tpu_custom_call" | custom-call | bytes 1048576 | tf_op jit(solution)/shard_map/unpack_rows/pallas_call | solution.py:268
  (8 shorter events, 0.1 us)
Async XLA Ops:
  0.1 1.2 %copy-start = (bf16[2,256,1024]{2,1,0:T(8,128)(2,1)S(1)}, bf16[2,256,1024]{2,1,0:T(8,128)(2,1)}, u32[]{:S(2)}) copy-start(bf16[2,256,1024]{2,1,0:T(8,128)(2,1)} %kv_ref.1) | copy-start | bytes 3145732
  1.3 2.8 %copy-start.1 = (bf16[2,24,5,512]{3,1,2,0:T(8,128)(2,1)S(1)}, bf16[2,24,5,512]{3,1,2,0:T(8,128)(2,1)}, u32[]{:S(2)}) copy-start(bf16[2,24,5,512]{3,1,2,0:T(8,128)(2,1)} %param.6) | copy-start | bytes 737284
  1.3 2.8 %copy-start.2 = (bf16[2,2,24,5,64]{4,2,3,1,0:T(8,128)(2,1)S(1)}, bf16[2,2,24,5,64]{4,2,3,1,0:T(8,128)(2,1)}, u32[]{:S(2)}) copy-start(bf16[2,2,24,5,64]{4,2,3,1,0:T(8,128)(2,1)} %param.8) | copy-start | bytes 184324
  2.1 15.5 %collective-permute-start = (bf16[2304,128]{1,0:T(8,128)(2,1)S(1)}, bf16[2304,128]{1,0:T(8,128)(2,1)S(1)}, u32[]{:S(2)}, u32[]{:S(2)}) collective-permute-start(bf16[2304,128]{1,0:T(8,128)(2,1)S(1)} %get-tuple-element.16.refs_0_), channel_id=1, source_target_pairs={{0,1},{1,0},{2,3},{3,2},{4,5},{5,4},{6,7},{7,6},{8,9},{9,8},{10,11... | collective-permute-start | bytes 1769480 | tf_op jit(solution)/shard_map/ppermute | solution.py:291
  4.1 0.7 copy-start.3
  6.6 38.8 %all-to-all-start = ((bf16[32,100,128]{2,1,0:T(8,128)(2,1)}), bf16[32,100,128]{2,1,0:T(8,128)(2,1)S(1)}, u32[]{:S(2)}, u32[]{:S(2)}) async-start(bf16[32,100,128]{2,1,0:T(8,128)(2,1)} %get-tuple-element.19), calls=%async_computation | async-start | bytes 1703936 | tf_op jit(solution)/shard_map/all_to_all | solution.py:315
  17.7 11.3 %copy-start.6 = (s32[1,24]{1,0:T(1,128)S(1)}, s32[1,24]{1,0:T(1,128)}, u32[]{:S(2)}) copy-start(s32[1,24]{1,0:T(1,128)} %param.9) | copy-start | bytes 292
  18.5 18.1 %copy-start.4 = (bf16[512,128]{1,0:T(8,128)(2,1)}, bf16[512,128]{1,0:T(8,128)(2,1)S(1)}, u32[]{:S(2)}) copy-start(bf16[512,128]{1,0:T(8,128)(2,1)S(1)} %get-tuple-element.26) | copy-start | bytes 393220
  18.5 10.6 %copy-start.5 = (s32[2,768]{1,0:T(2,128)S(1)}, s32[2,768]{1,0:T(2,128)}, u32[]{:S(2)}) copy-start(s32[2,768]{1,0:T(2,128)} %param.10) | copy-start | bytes 18436
  18.5 21.0 %collective-permute-start.1 = (bf16[1024,128]{1,0:T(8,128)(2,1)S(1)}, bf16[1024,128]{1,0:T(8,128)(2,1)S(1)}, u32[]{:S(2)}, u32[]{:S(2)}) collective-permute-start(bf16[1024,128]{1,0:T(8,128)(2,1)S(1)} %get-tuple-element.23), channel_id=1, source_target_pairs={{0,2},{1,15},{2,4},{3,1},{4,6},{5,3},{6,8},{7,5},{8,10},{9,7},{10,... | collective-permute-start | bytes 786440 | tf_op jit(solution)/shard_map/ppermute | solution.py:288
  22.9 19.8 %collective-permute-start.2 = (bf16[1024,128]{1,0:T(8,128)(2,1)S(1)}, bf16[1024,128]{1,0:T(8,128)(2,1)S(1)}, u32[]{:S(2)}, u32[]{:S(2)}) collective-permute-start(bf16[1024,128]{1,0:T(8,128)(2,1)S(1)} %get-tuple-element.24), channel_id=1, source_target_pairs={{0,4},{1,13},{2,6},{3,15},{4,8},{5,1},{6,10},{7,3},{8,12},{9,5},{1... | collective-permute-start | bytes 786440 | tf_op jit(solution)/shard_map/ppermute | solution.py:288
  29.2 24.4 %collective-permute-start.3 = (bf16[1024,128]{1,0:T(8,128)(2,1)}, bf16[1024,128]{1,0:T(8,128)(2,1)S(1)}, u32[]{:S(2)}, u32[]{:S(2)}) collective-permute-start(bf16[1024,128]{1,0:T(8,128)(2,1)} %get-tuple-element.25), channel_id=1, source_target_pairs={{0,6},{1,11},{2,8},{3,13},{4,10},{5,15},{6,12},{7,1},{8,14},{9,3},... | collective-permute-start | bytes 786440 | tf_op jit(solution)/shard_map/ppermute | solution.py:288
  36.6 16.9 %collective-permute-start.4 = (bf16[512,128]{1,0:T(8,128)(2,1)}, bf16[512,128]{1,0:T(8,128)(2,1)S(1)}, u32[]{:S(2)}, u32[]{:S(2)}) collective-permute-start(bf16[512,128]{1,0:T(8,128)(2,1)} %copy-done.4), channel_id=1, source_target_pairs={{0,8},{1,9},{2,10},{3,11},{4,12},{5,13},{6,14},{7,15},{8,0},{9,1},... | collective-permute-start | bytes 393224 | tf_op jit(solution)/shard_map/ppermute | solution.py:288
  43.5 12.1 %collective-permute-start.5 = (bf16[2048,128]{1,0:T(8,128)(2,1)}, bf16[2048,128]{1,0:T(8,128)(2,1)S(1)}, u32[]{:S(2)}, u32[]{:S(2)}) collective-permute-start(bf16[2048,128]{1,0:T(8,128)(2,1)} %pad_maximum_fusion), channel_id=1, source_target_pairs={{0,1},{1,0},{2,3},{3,2},{4,5},{5,4},{6,7},{7,6},{8,9},{9,8},{10,11... | collective-permute-start | bytes 1572872 | tf_op jit(solution)/shard_map/ppermute | solution.py:291
  53.7 3.8 %collective-permute-start.6 = (bf16[1920,128]{1,0:T(8,128)(2,1)S(1)}, bf16[1920,128]{1,0:T(8,128)(2,1)S(1)}, u32[]{:S(2)}, u32[]{:S(2)}) collective-permute-start(bf16[1920,128]{1,0:T(8,128)(2,1)S(1)} %pad_maximum_fusion.1), channel_id=1, source_target_pairs={{0,1},{1,0},{2,3},{3,2},{4,5},{5,4},{6,7},{7,6},{8,9},{9,8},{10,11... | collective-permute-start | bytes 1474568 | tf_op jit(solution)/shard_map/ppermute | solution.py:291

commit v5 on v4

--- a/solution.py
+++ b/solution.py
@@ -174,7 +174,7 @@
                     unit = 2 * half + side
                     there = core if half == 0 else 1 - core
                     place(1 + dist, unit, side, z - step * dist, there)
-                    far, at = (6, 4 * (dist - 1)) if dist < 3 else (7, 0)
+                    far, at = (7, 0) if dist == 2 else (6, 2 * (dist - 1))
                     place(far, at + unit, side, z + step * dist, 1 - there)
         for half in range(2):
             there = core if half == 0 else 1 - core
@@ -293,15 +293,16 @@
     keep, give = split_cache(jnp.stack([z, core]).astype(jnp.int32), kv_cache)
     got = sibling(give)
     moved = [along_z(x, k + 1) for k, x in enumerate(join_cores(keep, got))]
-    crossed_a = sibling(jnp.concatenate(moved[:2], axis=0))
-
-    group_of = dest // RD
+    crossed_a = sibling(jnp.concatenate([moved[0], moved[2]], axis=0))
+
     order = jnp.arange(RD)
-    here = (group_of == me_dp).reshape(n_dp, RD)
-    before = jnp.sum(here[:, None, :] & (order[None, :] < order[:, None]), axis=2)
-    place = (jnp.arange(n_dp)[:, None] * 2 + before).reshape(-1)
+    index = jnp.arange(dest.shape[0])
     hit = dest[None, :] == (me_dp * RD + order)[:, None]
-    recv_pos = jnp.sum(jnp.where(hit, place[None, :], 0), axis=1)
+    row = jnp.sum(jnp.where(hit, index[None, :], 0), axis=1)
+    source = row // RD
+    here = (dest >= me_dp * RD) & (dest < (me_dp + 1) * RD)
+    before = here[None, :] & (index[None, :] // RD == source[:, None]) & (index[None, :] < row[:, None])
+    recv_pos = source * 2 + jnp.sum(before, axis=1)
     taken = jnp.sum(jnp.where(hit[None], accepted[:, None, :], 0), axis=2)
     length = lengths[0]
     start = jnp.sum(jnp.where(order[None, :] < order[:, None], length[None, :], 0), axis=1)
@@ -314,7 +315,7 @@
     packed, send_pos = pack_rows(dest, first, *by_token)
     received = lax.all_to_all(packed, "dp", split_axis=0, concat_axis=0, tiled=True)
     rows, fresh = pick_rows(info, received)
-    crossed_b = sibling(jnp.concatenate(moved[2:] + [fresh], axis=0))
+    crossed_b = sibling(jnp.concatenate([moved[1], moved[3], fresh], axis=0))
     outs = attend(info, rows, fresh, [give, got] + moved + [crossed_a, crossed_b])
     back = lax.all_to_all(
         outs.reshape(n_dp, 2 * QR, HD), "dp", split_axis=0, concat_axis=0, tiled=True

time: 91.6 us -> 91.9 us (level)
  no operation moved by 1% of the time
where the time goes in v5:
time: 91.9 us; the launch traced here: 91.4 us
  starting transfers between devices  36.6 us (40%)
  blocking collectives  29.6 us (32%)
  waiting for transfers between devices  12.5 us (14%)
  Pallas kernels  8.24 us (9%)
  local copies, waits for them, and re-layouts  2.58 us (3%)
  other arithmetic  1.7 us (2%)
    all_to_all x1, blocking collectives, body(): lax.all_to_all(outs.reshape(n_dp, 2 * QR, HD), 'dp', split_axis=0, concat...  29.6 us
    ppermute x4, starting transfers between devices, along_z(): return lax.ppermute(x, 'tensor', perm)  20.6 us
    ppermute x4, waiting for transfers between devices, along_z(): return lax.ppermute(x, 'tensor', perm)  10.7 us
    all_to_all x1, starting transfers between devices, body(): lax.all_to_all(packed, 'dp', split_axis=0, concat_axis=0, tiled=True)  10.2 us
    ppermute x3, starting transfers between devices, sibling(): return lax.ppermute(x, 'tensor', [(t, t ^ 1) for t in range(16)])  5.75 us
    pallas_call x1, Pallas kernels, attend(): pl.pallas_call(kernel, out_shape=jax.ShapeDtypeStruct((64, QR, HD), jnp.b...  2.66 us
    unnamed x14, local copies, waits for them, and re-layouts  2.55 us
    pallas_call x1, Pallas kernels, pack_rows(): pl.pallas_call(kernel, out_shape=(jax.ShapeDtypeStruct((32, 2 * (QR + TOK...  1.89 us
  transfers between devices with their start and end apart: 8, of which 4 were waited for; matrix products, arithmetic and copies ran while one was open for 2% of the time, Pallas kernels for 4%

profile of v5, /device:TPU:8, one launch (start us, length us, event | category | flops | bytes accessed | tf_op | source)
XLA Modules:
  0.0 91.4 jit_solution(16669906503827752935)
XLA Ops:
  0.0 0.1 pad_add_fusion.id_ref
  0.1 0.0 copy-start
  0.1 1.2 %copy-done = bf16[2,256,1024]{2,1,0:T(8,128)(2,1)S(1)} copy-done((bf16[2,256,1024]{2,1,0:T(8,128)(2,1)S(1)}, bf16[2,256,1024]{2,1,0:T(8,128)(2,1)}, u32[]{:S(2)}) %copy-start) | copy-done | bytes 1048600
  1.3 0.0 copy-start.1
  1.3 0.0 copy-start.2
  1.3 0.8 split_cache.1
  2.1 1.9 %collective-permute-start = (bf16[2304,128]{1,0:T(8,128)(2,1)S(1)}, bf16[2304,128]{1,0:T(8,128)(2,1)S(1)}, u32[]{:S(2)}, u32[]{:S(2)}) collective-permute-start(bf16[2304,128]{1,0:T(8,128)(2,1)S(1)} %get-tuple-element.16.refs_0_), channel_id=1, source_target_pairs={{0,1},{1,0},{2,3},{3,2},{4,5},{5,4},{6,7},{7,6},{8,9},{9,8},{10,11... | collective-permute-start | bytes 1769480 | tf_op jit(solution)/shard_map/ppermute | solution.py:291
  4.1 0.0 copy-start.3
  4.1 0.0 copy-done.1
  4.1 0.0 copy-done.2
  4.1 0.7 copy-done.3
  4.8 1.9 %pack_rows.1 = (bf16[32,100,128]{2,1,0:T(8,128)(2,1)}, s32[24]{0:T(128)S(1)}) custom-call(s32[768]{0:T(1024)S(1)} %copy-done.3, s32[1]{0:T(128)} %bitcast.first_ref, bf16[2,5,24,512]{3,2,1,0:T(8,128)(2,1)S(1)} %bitcast.22, bf16[2,2,5,24,64]{4,3,2,1,0:T(8,128)(2,1)S(1)} %bitcast.23), custom_call_target="tpu_custom_call" | custom-call | bytes 2097152 | tf_op jit(solution)/shard_map/pack_rows/pallas_call | solution.py:103
  6.7 10.2 %all-to-all-start = ((bf16[32,100,128]{2,1,0:T(8,128)(2,1)}), bf16[32,100,128]{2,1,0:T(8,128)(2,1)S(1)}, u32[]{:S(2)}, u32[]{:S(2)}) async-start(bf16[32,100,128]{2,1,0:T(8,128)(2,1)} %get-tuple-element.19), calls=%async_computation | async-start | bytes 1703936 | tf_op jit(solution)/shard_map/all_to_all | solution.py:316
  16.8 0.2 select_reduce_fusion.1
  17.1 0.2 convert_reduce_fusion
  17.3 0.1 broadcast_compare_fusion
  17.4 0.0 collective-permute-done.got_ref.refs_1_
  17.4 0.8 join_cores.1
  18.2 0.0 copy-start.4
  18.2 0.7 copy-done.4
  18.8 0.0 copy-start.5
  18.8 4.4 %collective-permute-start.1 = (bf16[1024,128]{1,0:T(8,128)(2,1)S(1)}, bf16[1024,128]{1,0:T(8,128)(2,1)S(1)}, u32[]{:S(2)}, u32[]{:S(2)}) collective-permute-start(bf16[1024,128]{1,0:T(8,128)(2,1)S(1)} %get-tuple-element.23), channel_id=1, source_target_pairs={{0,2},{1,15},{2,4},{3,1},{4,6},{5,3},{6,8},{7,5},{8,10},{9,7},{10,... | collective-permute-start | bytes 786440 | tf_op jit(solution)/shard_map/ppermute | solution.py:288
  23.2 9.1 %collective-permute-start.3 = (bf16[1024,128]{1,0:T(8,128)(2,1)S(1)}, bf16[1024,128]{1,0:T(8,128)(2,1)S(1)}, u32[]{:S(2)}, u32[]{:S(2)}) collective-permute-start(bf16[1024,128]{1,0:T(8,128)(2,1)S(1)} %get-tuple-element.25), channel_id=1, source_target_pairs={{0,6},{1,11},{2,8},{3,13},{4,10},{5,15},{6,12},{7,1},{8,14},{9,3},... | collective-permute-start | bytes 786440 | tf_op jit(solution)/shard_map/ppermute | solution.py:288
  32.4 0.0 copy-done.5
  32.4 0.1 select_reduce_fusion
  32.5 0.0 copy-start.6
  32.5 4.3 %collective-permute-start.2 = (bf16[1024,128]{1,0:T(8,128)(2,1)}, bf16[1024,128]{1,0:T(8,128)(2,1)S(1)}, u32[]{:S(2)}, u32[]{:S(2)}) collective-permute-start(bf16[1024,128]{1,0:T(8,128)(2,1)} %get-tuple-element.24), channel_id=1, source_target_pairs={{0,4},{1,13},{2,6},{3,15},{4,8},{5,1},{6,10},{7,3},{8,12},{9,5},{1... | collective-permute-start | bytes 786440 | tf_op jit(solution)/shard_map/ppermute | solution.py:288
  36.8 0.0 copy-done.6
  36.8 0.1 select_reduce_fusion.2
  37.0 2.8 %collective-permute-start.4 = (bf16[512,128]{1,0:T(8,128)(2,1)}, bf16[512,128]{1,0:T(8,128)(2,1)S(1)}, u32[]{:S(2)}, u32[]{:S(2)}) collective-permute-start(bf16[512,128]{1,0:T(8,128)(2,1)} %copy-done.4), channel_id=1, source_target_pairs={{0,8},{1,9},{2,10},{3,11},{4,12},{5,13},{6,14},{7,15},{8,0},{9,1},... | collective-permute-start | bytes 393224 | tf_op jit(solution)/shard_map/ppermute | solution.py:288
  39.8 0.0 collective-permute-done.1.refs_2_
  39.8 2.7 %collective-permute-done.3.refs_4_ = bf16[1024,128]{1,0:T(8,128)(2,1)S(1)} collective-permute-done((bf16[1024,128]{1,0:T(8,128)(2,1)S(1)}, bf16[1024,128]{1,0:T(8,128)(2,1)S(1)}, u32[]{:S(2)}, u32[]{:S(2)}) %collective-permute-start.3) | collective-permute-done | bytes 262176 | tf_op jit(solution)/shard_map/ppermute | solution.py:288
  42.5 0.8 pad_maximum_fusion
  43.3 1.9 %collective-permute-start.5 = (bf16[2048,128]{1,0:T(8,128)(2,1)}, bf16[2048,128]{1,0:T(8,128)(2,1)S(1)}, u32[]{:S(2)}, u32[]{:S(2)}) collective-permute-start(bf16[2048,128]{1,0:T(8,128)(2,1)} %pad_maximum_fusion), channel_id=1, source_target_pairs={{0,1},{1,0},{2,3},{3,2},{4,5},{5,4},{6,7},{7,6},{8,9},{9,8},{10,11... | collective-permute-start | bytes 1572872 | tf_op jit(solution)/shard_map/ppermute | solution.py:291
  45.2 0.0 all-to-all-done.recv_ref
  45.3 0.8 pick_rows.1
  46.0 7.4 %collective-permute-done.4.refs_5_ = bf16[512,128]{1,0:T(8,128)(2,1)S(1)} collective-permute-done((bf16[512,128]{1,0:T(8,128)(2,1)}, bf16[512,128]{1,0:T(8,128)(2,1)S(1)}, u32[]{:S(2)}, u32[]{:S(2)}) %collective-permute-start.4) | collective-permute-done | bytes 131104 | tf_op jit(solution)/shard_map/ppermute | solution.py:288
  53.5 0.6 collective-permute-done.2.refs_3_
  54.1 1.9 %collective-permute-start.6 = (bf16[1920,128]{1,0:T(8,128)(2,1)S(1)}, bf16[1920,128]{1,0:T(8,128)(2,1)S(1)}, u32[]{:S(2)}, u32[]{:S(2)}) collective-permute-start(bf16[1920,128]{1,0:T(8,128)(2,1)S(1)} %pad_maximum_fusion.1), channel_id=1, source_target_pairs={{0,1},{1,0},{2,3},{3,2},{4,5},{5,4},{6,7},{7,6},{8,9},{9,8},{10,11... | collective-permute-start | bytes 1474568 | tf_op jit(solution)/shard_map/ppermute | solution.py:291
  56.0 0.0 collective-permute-done.5.refs_6_
  56.0 1.8 %collective-permute-done.6.refs_7_ = bf16[1920,128]{1,0:T(8,128)(2,1)S(1)} collective-permute-done((bf16[1920,128]{1,0:T(8,128)(2,1)S(1)}, bf16[1920,128]{1,0:T(8,128)(2,1)S(1)}, u32[]{:S(2)}, u32[]{:S(2)}) %collective-permute-start.6) | collective-permute-done | bytes 491552 | tf_op jit(solution)/shard_map/ppermute | solution.py:291
  57.8 2.7 %attend.1 = bf16[64,40,128]{2,1,0:T(8,128)(2,1)S(1)} custom-call(s32[6,24]{1,0:T(8,128)S(1)} %stack.21.info_ref, bf16[24,40,128]{2,1,0:T(8,128)(2,1)S(1)} %get-tuple-element.20.qs, bf16[384,128]{1,0:T(8,128)(2,1)S(1)} %get-tuple-element.21.fresh_ref, bf16[2304,128]{1,0:T(8,128)(2,1)S(1)} %get-tuple-element.16.refs_0_, ...), custom_call_target="tpu_custom_call" | custom-call | flops 294912000 | bytes 4194304 | tf_op jit(solution)/shard_map/attend/pallas_call | solution.py:235
  60.5 29.6 %all_to_all.10 = bf16[32,80,128]{2,1,0:T(8,128)(2,1)S(1)} all-to-all(bf16[32,80,128]{2,1,0:T(8,128)(2,1)S(1)} %bitcast.20), channel_id=1, replica_groups=mesh['dp'=32,'tensor'=16] {'dp'}, dimensions={0} | all-to-all | bytes 1310720 | tf_op jit(solution)/shard_map/all_to_all | solution.py:320
  90.1 1.4 %unpack_rows.1 = bf16[2,5,24,512]{3,2,1,0:T(8,128)(2,1)} custom-call(s32[24]{0:T(128)S(1)} %get-tuple-element.18.pos_ref, bf16[64,40,128]{2,1,0:T(8,128)(2,1)S(1)} %bitcast.21), custom_call_target="tpu_custom_call" | custom-call | bytes 1048576 | tf_op jit(solution)/shard_map/unpack_rows/pallas_call | solution.py:268
  (7 shorter events, 0.1 us)
Async XLA Ops:
  0.1 1.2 %copy-start = (bf16[2,256,1024]{2,1,0:T(8,128)(2,1)S(1)}, bf16[2,256,1024]{2,1,0:T(8,128)(2,1)}, u32[]{:S(2)}) copy-start(bf16[2,256,1024]{2,1,0:T(8,128)(2,1)} %kv_ref.1) | copy-start | bytes 3145732
  1.3 2.8 %copy-start.1 = (bf16[2,24,5,512]{3,1,2,0:T(8,128)(2,1)S(1)}, bf16[2,24,5,512]{3,1,2,0:T(8,128)(2,1)}, u32[]{:S(2)}) copy-start(bf16[2,24,5,512]{3,1,2,0:T(8,128)(2,1)} %param.6) | copy-start | bytes 737284
  1.3 2.8 %copy-start.2 = (bf16[2,2,24,5,64]{4,2,3,1,0:T(8,128)(2,1)S(1)}, bf16[2,2,24,5,64]{4,2,3,1,0:T(8,128)(2,1)}, u32[]{:S(2)}) copy-start(bf16[2,2,24,5,64]{4,2,3,1,0:T(8,128)(2,1)} %param.8) | copy-start | bytes 184324
  2.1 15.2 %collective-permute-start = (bf16[2304,128]{1,0:T(8,128)(2,1)S(1)}, bf16[2304,128]{1,0:T(8,128)(2,1)S(1)}, u32[]{:S(2)}, u32[]{:S(2)}) collective-permute-start(bf16[2304,128]{1,0:T(8,128)(2,1)S(1)} %get-tuple-element.16.refs_0_), channel_id=1, source_target_pairs={{0,1},{1,0},{2,3},{3,2},{4,5},{5,4},{6,7},{7,6},{8,9},{9,8},{10,11... | collective-permute-start | bytes 1769480 | tf_op jit(solution)/shard_map/ppermute | solution.py:291
  4.1 0.7 copy-start.3
  6.7 38.6 %all-to-all-start = ((bf16[32,100,128]{2,1,0:T(8,128)(2,1)}), bf16[32,100,128]{2,1,0:T(8,128)(2,1)S(1)}, u32[]{:S(2)}, u32[]{:S(2)}) async-start(bf16[32,100,128]{2,1,0:T(8,128)(2,1)} %get-tuple-element.19), calls=%async_computation | async-start | bytes 1703936 | tf_op jit(solution)/shard_map/all_to_all | solution.py:316
  18.2 0.7 copy-start.4
  18.8 13.5 %copy-start.5 = (s32[2,768]{1,0:T(2,128)S(1)}, s32[2,768]{1,0:T(2,128)}, u32[]{:S(2)}) copy-start(s32[2,768]{1,0:T(2,128)} %param.10) | copy-start | bytes 18436
  18.8 21.0 %collective-permute-start.1 = (bf16[1024,128]{1,0:T(8,128)(2,1)S(1)}, bf16[1024,128]{1,0:T(8,128)(2,1)S(1)}, u32[]{:S(2)}, u32[]{:S(2)}) collective-permute-start(bf16[1024,128]{1,0:T(8,128)(2,1)S(1)} %get-tuple-element.23), channel_id=1, source_target_pairs={{0,2},{1,15},{2,4},{3,1},{4,6},{5,3},{6,8},{7,5},{8,10},{9,7},{10,... | collective-permute-start | bytes 786440 | tf_op jit(solution)/shard_map/ppermute | solution.py:288
  23.2 19.3 %collective-permute-start.3 = (bf16[1024,128]{1,0:T(8,128)(2,1)S(1)}, bf16[1024,128]{1,0:T(8,128)(2,1)S(1)}, u32[]{:S(2)}, u32[]{:S(2)}) collective-permute-start(bf16[1024,128]{1,0:T(8,128)(2,1)S(1)} %get-tuple-element.25), channel_id=1, source_target_pairs={{0,6},{1,11},{2,8},{3,13},{4,10},{5,15},{6,12},{7,1},{8,14},{9,3},... | collective-permute-start | bytes 786440 | tf_op jit(solution)/shard_map/ppermute | solution.py:288
  32.5 4.3 %copy-start.6 = (s32[1,24]{1,0:T(1,128)S(1)}, s32[1,24]{1,0:T(1,128)}, u32[]{:S(2)}) copy-start(s32[1,24]{1,0:T(1,128)} %param.9) | copy-start | bytes 292
  32.5 21.5 %collective-permute-start.2 = (bf16[1024,128]{1,0:T(8,128)(2,1)}, bf16[1024,128]{1,0:T(8,128)(2,1)S(1)}, u32[]{:S(2)}, u32[]{:S(2)}) collective-permute-start(bf16[1024,128]{1,0:T(8,128)(2,1)} %get-tuple-element.24), channel_id=1, source_target_pairs={{0,4},{1,13},{2,6},{3,15},{4,8},{5,1},{6,10},{7,3},{8,12},{9,5},{1... | collective-permute-start | bytes 786440 | tf_op jit(solution)/shard_map/ppermute | solution.py:288
  37.0 16.5 %collective-permute-start.4 = (bf16[512,128]{1,0:T(8,128)(2,1)}, bf16[512,128]{1,0:T(8,128)(2,1)S(1)}, u32[]{:S(2)}, u32[]{:S(2)}) collective-permute-start(bf16[512,128]{1,0:T(8,128)(2,1)} %copy-done.4), channel_id=1, source_target_pairs={{0,8},{1,9},{2,10},{3,11},{4,12},{5,13},{6,14},{7,15},{8,0},{9,1},... | collective-permute-start | bytes 393224 | tf_op jit(solution)/shard_map/ppermute | solution.py:288
  43.3 12.7 %collective-permute-start.5 = (bf16[2048,128]{1,0:T(8,128)(2,1)}, bf16[2048,128]{1,0:T(8,128)(2,1)S(1)}, u32[]{:S(2)}, u32[]{:S(2)}) collective-permute-start(bf16[2048,128]{1,0:T(8,128)(2,1)} %pad_maximum_fusion), channel_id=1, source_target_pairs={{0,1},{1,0},{2,3},{3,2},{4,5},{5,4},{6,7},{7,6},{8,9},{9,8},{10,11... | collective-permute-start | bytes 1572872 | tf_op jit(solution)/shard_map/ppermute | solution.py:291
  54.1 3.8 %collective-permute-start.6 = (bf16[1920,128]{1,0:T(8,128)(2,1)S(1)}, bf16[1920,128]{1,0:T(8,128)(2,1)S(1)}, u32[]{:S(2)}, u32[]{:S(2)}) collective-permute-start(bf16[1920,128]{1,0:T(8,128)(2,1)S(1)} %pad_maximum_fusion.1), channel_id=1, source_target_pairs={{0,1},{1,0},{2,3},{3,2},{4,5},{5,4},{6,7},{7,6},{8,9},{9,8},{10,11... | collective-permute-start | bytes 1474568 | tf_op jit(solution)/shard_map/ppermute | solution.py:291
